TPU v7x, 32 devices: a whole 2x2x4 slice. The times are simulated.
32 devices in a mesh: rows: 8 (over z, core), seq: 4 (over y, x).
Axes of the slice: x: 2, y: 2, z: 4, core: 2. Of those that a mesh axis runs over, the one named last changes fastest.
Arguments:
- tokens: bfloat16 [16, 1024, 1152], P('rows', 'seq'), may hold values from -6 to 6
- conditioning: bfloat16 [128, 1152], P('rows'), may hold values from -6 to 6
- segment_ids: int32 [16, 1024], P('rows'), may hold values from 0 to 7, as said below
- image_index: int32 [16, 8], P('rows'), may hold values from 0 to 15
- row_fill: int32 [16], P('rows'), may hold values from 512 to 1024, as said below
- ada_weight: bfloat16 [1152, 6912], P(None, 'seq'), may hold values from -0.1875 to 0.1875
- ada_bias: bfloat16 [6912], replicated, may hold values from -1.796875 to 1.796875
- qkv_weight: bfloat16 [1152, 3456], replicated, may hold values from -0.1875 to 0.1875
- qv_bias: bfloat16 [2, 1152], replicated, may hold values from -1.796875 to 1.796875
- proj_weight: bfloat16 [1152, 1152], replicated, may hold values from -2 to 2
- proj_bias: bfloat16 [1152], replicated, may hold values from -1.796875 to 1.796875
- up_weight: bfloat16 [1152, 4608], replicated, may hold values from -0.1875 to 0.1875
- up_bias: bfloat16 [4608], replicated, may hold values from -1.796875 to 1.796875
- down_weight: bfloat16 [4608, 1152], replicated, may hold values from -0.09375 to 0.09375
- down_bias: bfloat16 [1152], replicated, may hold values from -1.796875 to 1.796875
- cotangent: bfloat16 [16, 1024, 1152], P('rows', 'seq'), may hold values from -6 to 6
Outputs:
- block_out: bfloat16 [16, 1024, 1152], P('rows', 'seq')
- grad_tokens: float32 [16, 1024, 1152], P('rows', 'seq')
- grad_cond: float32 [128, 1152], P('rows')
- grad_ada_weight: float32 [1152, 6912], P('rows', 'seq')
- grad_ada_bias: float32 [6912], replicated
- grad_qkv_weight: float32 [1152, 3456], P('rows', 'seq')
- grad_qv_bias: float32 [2, 1152], replicated
- grad_proj_weight: float32 [1152, 1152], P('rows', 'seq')
- grad_proj_bias: float32 [1152], replicated
- grad_up_weight: float32 [1152, 4608], P('rows', 'seq')
- grad_up_bias: float32 [4608], replicated
- grad_down_weight: float32 [4608, 1152], P('rows', 'seq')
- grad_down_bias: float32 [1152], replicated
Inputs may be any that keep to these rules, and one draw needn't show every extreme that they name: `segment_ids`: never falls along a row; in every aligned block of 2 rows one row has a segment that holds every position from 1024 // (2 * 4) to 1024 - 1024 // (2 * 4). `row_fill`: that row's fill is above 1024 - 1024 // (2 * 4).
All inputs are finite; a program needn't handle non-finite values.
Results may differ from a plain program's by a relative error of at most 0.012.
The roundings to bfloat16 on the way count: a program that leaves them out, or rounds other values in their place, can miss the bound.
Values may be sent and summed in bfloat16 or wider, within the bound.
A program may use at most 256 MiB of HBM per device.

v0:
```python
from functools import partial
import math

import jax
import jax.numpy as jnp
from jax import lax
from jax.experimental import pallas as pl
from jax.experimental.pallas import tpu as pltpu
from jax.sharding import PartitionSpec as P

HEADS = 16
LOG2E = math.log2(math.e)
VMEM_LIMIT = 60 << 20
BF16 = jnp.bfloat16
F32 = jnp.float32

norm_eps = 1e-06


def modulate(values, offset, factor):
    center = values - jnp.mean(values, axis=-1, keepdims=True)
    spread = jnp.mean(center * center, axis=-1, keepdims=True)
    return center * lax.rsqrt(spread + norm_eps) * (1.0 + factor) + offset


def gelu_tanh(values):
    return jax.nn.gelu(values, approximate=True)


def swap(values, axis, mask):
    count = lax.axis_size(axis)
    return lax.ppermute(values, axis, [(i, i ^ mask) for i in range(count)])


def flip_blocks(values, axis, mask):
    return jnp.take(values, lax.iota(jnp.int32, values.shape[axis]) ^ mask, axis=axis)


def qkv_kernel(slot_row, seg, mod, tokens, weight, bias, normed_ref, qkv_ref):
    width = tokens.shape[-1]
    values = tokens[0].astype(F32)
    picked = (seg[0] == slot_row[...]).astype(BF16)
    table = mod[0]
    high = table.astype(BF16)
    rest = table - high.astype(F32)
    middle = rest.astype(BF16)
    last = (rest - middle.astype(F32)).astype(BF16)
    stacked = jnp.concatenate([high, middle, last], axis=0)
    per_token = jnp.dot(picked, stacked, preferred_element_type=F32)
    normed = modulate(values, per_token[:, :width], per_token[:, width:]).astype(BF16)
    normed_ref[0] = normed
    mixed = lax.dot_general(weight[...], normed, (((1,), (1,)), ((), ())), preferred_element_type=F32)
    mixed = (mixed + bias[...]).astype(BF16)
    _, parts, heads, size, _ = qkv_ref.shape
    for part in range(parts):
        for head in range(heads):
            start = (part * heads + head) * size
            qkv_ref[0, part, head] = mixed[start : start + size]


def project_qkv(tokens, seg, slot_mod, weight, bias, heads, block):
    rows, length, width = tokens.shape
    slots = slot_mod.shape[1]
    features = weight.shape[0]
    size = features // (3 * heads)
    slot_row = jnp.tile(lax.iota(jnp.int32, slots), 3)[None]
    return pl.pallas_call(
        qkv_kernel,
        grid=(rows, length // block),
        in_specs=[
            pl.BlockSpec((1, 3 * slots), lambda r, t: (0, 0)),
            pl.BlockSpec((1, block, 1), lambda r, t: (r, t, 0)),
            pl.BlockSpec((1, slots, 2 * width), lambda r, t: (r, 0, 0)),
            pl.BlockSpec((1, block, width), lambda r, t: (r, t, 0)),
            pl.BlockSpec((features, width), lambda r, t: (0, 0)),
            pl.BlockSpec((features, 1), lambda r, t: (0, 0)),
        ],
        out_specs=[
            pl.BlockSpec((1, block, width), lambda r, t: (r, t, 0)),
            pl.BlockSpec((1, 3, heads, size, block), lambda r, t: (r, 0, 0, 0, t)),
        ],
        out_shape=[
            jax.ShapeDtypeStruct((rows, length, width), BF16),
            jax.ShapeDtypeStruct((rows, 3, heads, size, length), BF16),
        ],
        compiler_params=pltpu.CompilerParams(vmem_limit_bytes=VMEM_LIMIT),
        cost_estimate=pl.CostEstimate(
            flops=2 * rows * length * width * features,
            bytes_accessed=2 * rows * length * (2 * width + features),
            transcendentals=0,
        ),
    )(slot_row, seg[:, :, None], slot_mod, tokens, weight, bias[:, None])


def peers_of(seq):
    x, y = lax.rem(seq, 2), lax.div(seq, 2)
    return [seq + 1 - 2 * x, seq + 2 - 4 * y, 3 - seq]


def greet(devices):
    barrier = pltpu.get_barrier_semaphore()
    for device in devices:
        pl.semaphore_signal(barrier, inc=1, device_id=device, device_id_type=pl.DeviceIdType.MESH)
    pl.semaphore_wait(barrier, len(devices))


def send_block(source, target, sent, came, index, device):
    return pltpu.make_async_remote_copy(
        src_ref=source,
        dst_ref=target,
        send_sem=sent.at[index],
        recv_sem=came.at[index],
        device_id=device,
        device_id_type=pl.DeviceIdType.MESH,
    )


def attend_kernel(block, scale, code_col, code_row, query, key, value, out_ref, lse_ref, token_ref=None, sent=None, came=None, kept=None):
    length = query.shape[-1]
    keys = key[0, 0].astype(F32).T.astype(BF16)
    values = value[0, 0]
    codes = code_col[0]
    row, head = (pl.program_id(0), pl.program_id(1)) if sent is not None else (0, 0)
    rows, heads = out_ref.shape[:2]
    if sent is not None:
        seq = lax.axis_index("seq")
        peers = peers_of(seq)
        size = length // 4

        @pl.when((row == 0) & (head == 0))
        def _():
            greet([{"seq": peer} for peer in peers])

        def to_peer(r, h, m):
            lanes = pl.ds(m * size, size)
            place = (r * heads + h) * 3 + m - 1
            return send_block(out_ref.at[r, h, :, lanes], token_ref.at[r, seq, h], sent, came, place, {"seq": peers[m - 1]})

        def to_self(r, h):
            return pltpu.make_async_copy(out_ref.at[r, h, :, pl.ds(0, size)], token_ref.at[r, seq, h], kept.at[r * heads + h])

    for step in range(length // block):
        here = pl.ds(step * block, block)
        scores = jnp.dot(keys, query[0, 0, :, here], preferred_element_type=F32)
        scores = jnp.where(codes == code_row[0, :, here], scores * scale, -1e30)
        peak = jnp.max(scores, axis=0, keepdims=True)
        raised = jnp.exp2(scores - peak)
        total = jnp.sum(raised, axis=0, keepdims=True)
        probs = (raised * (1.0 / total)).astype(BF16)
        out_ref[row, head, :, here] = jnp.dot(values, probs, preferred_element_type=F32).astype(BF16)
        lse_ref[0, 0, :, here] = peak + jnp.log2(total)

    if sent is not None:
        to_self(row, head).start()
        for m in range(1, 4):
            to_peer(row, head, m).start()

        @pl.when((row == rows - 1) & (head == heads - 1))
        def _():
            for r in range(rows):
                for h in range(heads):
                    to_self(r, h).wait()
                    for m in range(1, 4):
                        to_peer(r, h, m).wait()


def attend(packed, col, row, block, exchange):
    rows, _, heads, size, length = packed.shape
    part = lambda j: pl.BlockSpec((1, None, 1, size, length), lambda r, h: (r, j, h, 0, 0))
    out_specs = [
        pl.BlockSpec((1, 1, size, length), lambda r, h: (r, h, 0, 0)),
        pl.BlockSpec((1, 1, 1, length), lambda r, h: (r, h, 0, 0)),
    ]
    out_shape = [
        jax.ShapeDtypeStruct((rows, heads, size, length), BF16),
        jax.ShapeDtypeStruct((rows, heads, 1, length), F32),
    ]
    scratch = []
    extra = {}
    if exchange:
        out_specs[0] = pl.BlockSpec((rows, heads, size, length), lambda r, h: (0, 0, 0, 0))
        out_specs.append(pl.BlockSpec(memory_space=pl.ANY))
        out_shape.append(jax.ShapeDtypeStruct((rows, 4, heads, size, length // 4), BF16))
        count = rows * heads
        scratch = [pltpu.SemaphoreType.DMA((3 * count,)), pltpu.SemaphoreType.DMA((3 * count,)), pltpu.SemaphoreType.DMA((count,))]
        extra = dict(collective_id=2, has_side_effects=True)
    return pl.pallas_call(
        partial(attend_kernel, block, size**-0.5 * LOG2E),
        grid=(rows, heads),
        in_specs=[
            pl.BlockSpec((1, length, 1), lambda r, h: (r, 0, 0)),
            pl.BlockSpec((1, 1, length), lambda r, h: (r, 0, 0)),
            part(0),
            part(1),
            part(2),
        ],
        out_specs=out_specs,
        out_shape=out_shape,
        scratch_shapes=scratch,
        compiler_params=pltpu.CompilerParams(vmem_limit_bytes=VMEM_LIMIT, **extra),
        cost_estimate=pl.CostEstimate(
            flops=8 * rows * heads * length * length * 128,
            bytes_accessed=8 * rows * heads * length * size,
            transcendentals=rows * heads * length * length,
        ),
    )(col, row, packed, packed, packed)


def attend_back_kernel(
    block,
    inner,
    scale,
    exchange,
    code_col,
    code_row,
    query,
    key,
    value,
    out,
    grad_out,
    lse,
    grad_ref,
    *rest,
):
    length = query.shape[-1]
    size = query.shape[-2]
    row, head = (pl.program_id(0), pl.program_id(1)) if exchange else (0, 0)
    rows, _, heads = grad_ref.shape[:3]
    if exchange:
        token_ref, key_sum, value_sum, keys, values, sent, came, kept = rest
        seq = lax.axis_index("seq")
        peers = peers_of(seq)
        local = length // 4

        @pl.when((row == 0) & (head == 0))
        def _():
            greet([{"seq": peer} for peer in peers])

        def to_peer(r, h, m):
            lanes = pl.ds(m * local, local)
            place = (r * heads + h) * 3 + m - 1
            return send_block(grad_ref.at[r, :, h, :, lanes], token_ref.at[r, :, seq, h], sent, came, place, {"seq": peers[m - 1]})

        def to_self(r, h):
            lanes = pl.ds(0, local)
            return pltpu.make_async_copy(grad_ref.at[r, :, h, :, lanes], token_ref.at[r, :, seq, h], kept.at[r * heads + h])

    else:
        key_sum, value_sum, keys, values = rest
    keys[...] = key[0, 0].astype(F32).T.astype(BF16)
    values[...] = value[0, 0].astype(F32).T.astype(BF16)
    for step in range(length // block):
        here = pl.ds(step * block, block)
        query_low = query[0, 0, :, here]
        grad_low = grad_out[0, 0, :, here]
        query_rows = query_low.astype(F32).T.astype(BF16)
        grad_rows = grad_low.astype(F32).T.astype(BF16)
        row_dot = jnp.sum(grad_low.astype(F32) * out[0, 0, :, here].astype(F32), axis=0, keepdims=True)
        grad_query = jnp.zeros((size, block), F32)
        for part in range(length // inner):
            there = pl.ds(part * inner, inner)
            scores = jnp.dot(keys[there, :], query_low, preferred_element_type=F32)
            scores = jnp.where(code_col[0, there, :] == code_row[0, :, here], scores * (scale * LOG2E), -1e30)
            probs = jnp.exp2(scores - lse[0, 0, :, here])
            grad_probs = jnp.dot(values[there, :], grad_low, preferred_element_type=F32)
            grad_raw = (probs * (grad_probs - row_dot) * scale).astype(BF16)
            value_part = jnp.dot(probs.astype(BF16), grad_rows, preferred_element_type=F32)
            key_part = jnp.dot(grad_raw, query_rows, preferred_element_type=F32)
            if step == 0:
                value_sum[there, :] = value_part
                key_sum[there, :] = key_part
            else:
                value_sum[there, :] += value_part
                key_sum[there, :] += key_part
            grad_query += jnp.dot(key[0, 0, :, there], grad_raw, preferred_element_type=F32)
        grad_ref[row, 0, head, :, here] = grad_query.astype(BF16)
    grad_ref[row, 1, head] = key_sum[...].T.astype(BF16)
    grad_ref[row, 2, head] = value_sum[...].T.astype(BF16)

    if exchange:
        to_self(row, head).start()
        for m in range(1, 4):
            to_peer(row, head, m).start()

        @pl.when((row == rows - 1) & (head == heads - 1))
        def _():
            for r in range(rows):
                for h in range(heads):
                    to_self(r, h).wait()
                    for m in range(1, 4):
                        to_peer(r, h, m).wait()


def attend_back(packed, out, grad_out, lse, col, row, block, inner, exchange):
    rows, _, heads, size, length = packed.shape
    part = lambda j: pl.BlockSpec((1, None, 1, size, length), lambda r, h: (r, j, h, 0, 0))
    whole = pl.BlockSpec((1, 1, size, length), lambda r, h: (r, h, 0, 0))
    out_specs = [pl.BlockSpec((1, 3, 1, size, length), lambda r, h: (r, 0, h, 0, 0))]
    out_shape = [jax.ShapeDtypeStruct((rows, 3, heads, size, length), BF16)]
    scratch = []
    extra = {}
    if exchange:
        out_specs = [
            pl.BlockSpec((rows, 3, heads, size, length), lambda r, h: (0, 0, 0, 0, 0)),
            pl.BlockSpec(memory_space=pl.ANY),
        ]
        out_shape.append(jax.ShapeDtypeStruct((rows, 3, 4, heads, size, length // 4), BF16))
        count = rows * heads
        scratch = [pltpu.SemaphoreType.DMA((3 * count,)), pltpu.SemaphoreType.DMA((3 * count,)), pltpu.SemaphoreType.DMA((count,))]
        extra = dict(collective_id=3, has_side_effects=True)
    return pl.pallas_call(
        partial(attend_back_kernel, block, inner, size**-0.5, exchange),
        grid=(rows, heads),
        in_specs=[
            pl.BlockSpec((1, length, 1), lambda r, h: (r, 0, 0)),
            pl.BlockSpec((1, 1, length), lambda r, h: (r, 0, 0)),
            part(0),
            part(1),
            part(2),
            whole,
            whole,
            pl.BlockSpec((1, 1, 1, length), lambda r, h: (r, h, 0, 0)),
        ],
        out_specs=out_specs,
        out_shape=out_shape,
        scratch_shapes=[
            pltpu.VMEM((length, size), F32),
            pltpu.VMEM((length, size), F32),
            pltpu.VMEM((length, size), BF16),
            pltpu.VMEM((length, size), BF16),
        ]
        + scratch,
        compiler_params=pltpu.CompilerParams(vmem_limit_bytes=VMEM_LIMIT, **extra),
        cost_estimate=pl.CostEstimate(
            flops=20 * rows * heads * length * length * 128,
            bytes_accessed=16 * rows * heads * length * size,
            transcendentals=rows * heads * length * length,
        ),
    )(col, row, packed, packed, packed, out, grad_out, lse)


def mlp_kernel(
    normed, grad_out, normed_turned, grad_turned, up, down, bias, out_sum, grad_sum, up_keep, up_send, down_keep, down_send, bias_sum
):
    step = pl.program_id(0)
    half = up_keep.shape[0]
    c0 = math.sqrt(2 / math.pi)
    c1 = c0 * 0.044715
    hidden = jnp.dot(normed[...], up[...], preferred_element_type=F32) + bias[...]
    square = hidden * hidden
    gate = 0.5 + 0.5 * jnp.tanh(hidden * (c0 + c1 * square))
    raised = hidden * gate
    slope = gate + raised * (1.0 - gate) * (2 * c0 + 6 * c1 * square)
    active = raised.astype(BF16)
    back = (((1,), (1,)), ((), ()))
    grad_active = lax.dot_general(grad_out[...], down[...], back, preferred_element_type=F32)
    grad_wide = (grad_active * slope).astype(BF16)
    out_part = jnp.dot(active, down[...], preferred_element_type=F32)
    grad_part = lax.dot_general(grad_wide, up[...], back, preferred_element_type=F32)

    @pl.when(step == 0)
    def _():
        out_sum[...] = out_part
        grad_sum[...] = grad_part

    @pl.when(step > 0)
    def _():
        out_sum[...] += out_part
        grad_sum[...] += grad_part

    bias_sum[...] = jnp.sum(grad_wide.astype(F32), axis=0, keepdims=True)
    up_keep[...] = jnp.dot(normed_turned[:half], grad_wide, preferred_element_type=F32)
    up_send[...] = jnp.dot(normed_turned[half:], grad_wide, preferred_element_type=F32).astype(BF16)
    down_keep[...] = jnp.dot(grad_turned[:half], active, preferred_element_type=F32)
    down_send[...] = jnp.dot(grad_turned[half:], active, preferred_element_type=F32).astype(BF16)


def feed_forward(normed, grad_out, normed_turned, grad_turned, up, down, bias, tile):
    count, width = normed.shape
    hidden = up.shape[1]
    half = width // 2
    fixed = lambda *shape: pl.BlockSpec(shape, lambda t: (0, 0))
    across = lambda rows: pl.BlockSpec((rows, tile), lambda t: (0, t))
    shape = jax.ShapeDtypeStruct
    return pl.pallas_call(
        mlp_kernel,
        grid=(hidden // tile,),
        in_specs=[
            fixed(count, width),
            fixed(count, width),
            fixed(width, count),
            fixed(width, count),
            across(width),
            pl.BlockSpec((tile, width), lambda t: (t, 0)),
            across(1),
        ],
        out_specs=[fixed(count, width), fixed(count, width), across(half), across(half), across(half), across(half), across(1)],
        out_shape=[
            shape((count, width), F32),
            shape((count, width), F32),
            shape((half, hidden), F32),
            shape((half, hidden), BF16),
            shape((half, hidden), F32),
            shape((half, hidden), BF16),
            shape((1, hidden), F32),
        ],
        compiler_params=pltpu.CompilerParams(vmem_limit_bytes=VMEM_LIMIT),
        cost_estimate=pl.CostEstimate(
            flops=12 * count * width * hidden,
            bytes_accessed=10 * width * hidden,
            transcendentals=count * hidden,
        ),
    )(normed, grad_out, normed_turned, grad_turned, up, down, bias)


def turn_halves(values, groups, mine):
    count, width = values.shape
    view = values.T.reshape(groups, 2, width // (2 * groups), count)
    keep = lax.dynamic_index_in_dim(view, mine, 1, keepdims=False).reshape(width // 2, count)
    send = lax.dynamic_index_in_dim(view, 1 - mine, 1, keepdims=False).reshape(width // 2, count)
    return jnp.concatenate([keep, send], axis=0)


STAGES = 4


def mlp_reduce_kernel(
    tiles,
    normed,
    grad_out,
    normed_turned,
    grad_turned,
    up0,
    up1,
    up2,
    up3,
    down0,
    down1,
    down2,
    down3,
    bias,
    out_sum,
    grad_sum,
    bias_sum,
    up_total,
    down_total,
    up_mine,
    down_mine,
    up_core,
    down_core,
    up_core_got,
    down_core_got,
    up_half,
    down_half,
    up_out,
    down_out,
    up_got,
    down_got,
    up_quarter,
    down_quarter,
    up_last,
    down_last,
    up_last_got,
    down_last_got,
    chip_full,
    chip_out,
    chip_got,
    core_sent,
    core_came,
    seq_sent,
    seq_came,
    last_sent,
    last_came,
    chip_sent,
    chip_came,
):
    step = pl.program_id(0)
    seq, row = lax.axis_index("seq"), lax.axis_index("rows")
    half = normed_turned.shape[0] // 2
    x, y = lax.rem(seq, 2), lax.div(seq, 2)
    core_peer = {"rows": row + 1 - 2 * lax.rem(row, 2)}
    x_peer = {"seq": seq + 1 - 2 * x}
    y_peer = {"seq": seq + 2 - 4 * y}
    chip, core = lax.div(row, 2), lax.rem(row, 2)
    to_chip = [lax.rem(chip + k, 4) for k in range(4)]
    chip_peers = [{"rows": 2 * to_chip[k] + core} for k in range(4)]

    @pl.when(step == 0)
    def _():
        barrier = pltpu.get_barrier_semaphore()
        for peer in (core_peer, x_peer, y_peer, *chip_peers[1:]):
            pl.semaphore_signal(barrier, inc=1, device_id=peer, device_id_type=pl.DeviceIdType.MESH)
        pl.semaphore_wait(barrier, 6)

    def copies(source, target, sent, came, slot, kind, device):
        return pltpu.make_async_remote_copy(
            src_ref=source.at[slot],
            dst_ref=target.at[slot],
            send_sem=sent.at[kind, slot],
            recv_sem=came.at[kind, slot],
            device_id=device,
            device_id_type=pl.DeviceIdType.MESH,
        )

    def to_core(slot):
        return (
            copies(up_core, up_core_got, core_sent, core_came, slot, 0, core_peer),
            copies(down_core, down_core_got, core_sent, core_came, slot, 1, core_peer),
        )

    def to_seq(slot):
        return (
            copies(up_out, up_got, seq_sent, seq_came, slot, 0, x_peer),
            copies(down_out, down_got, seq_sent, seq_came, slot, 1, y_peer),
        )

    def to_last(slot):
        return (
            copies(up_last, up_last_got, last_sent, last_came, slot, 0, y_peer),
            copies(down_last, down_last_got, last_sent, last_came, slot, 1, x_peer),
        )

    def to_chips(slot):
        return [
            pltpu.make_async_remote_copy(
                src_ref=chip_out.at[slot, to_chip[k]],
                dst_ref=chip_got.at[slot, k - 1],
                send_sem=chip_sent.at[k - 1, slot],
                recv_sem=chip_came.at[k - 1, slot],
                device_id=chip_peers[k],
                device_id_type=pl.DeviceIdType.MESH,
            )
            for k in range(1, 4)
        ]

    @pl.when(step >= 4)
    def _():
        slot = lax.rem(step, 2)
        for copy in to_chips(slot):
            copy.wait()
        for kind, total in enumerate((up_total, down_total)):
            value = chip_full[slot, chip, kind]
            for k in range(3):
                value = value + chip_got[slot, k, kind].astype(F32)
            total[...] = value

    @pl.when((step >= 3) & (step < tiles + 3))
    def _():
        slot = lax.rem(step + 1, 2)
        for copy in to_last(slot):
            copy.wait()
        size = half // 4
        ups = up_quarter[slot] + up_last_got[slot].astype(F32)
        downs = down_quarter[slot] + down_last_got[slot].astype(F32)
        for place in range(4):
            up_block = ups[place * size : (place + 1) * size]
            down_block = downs[:, place * 128 : (place + 1) * 128]
            chip_full[slot, place, 0] = up_block
            chip_full[slot, place, 1] = down_block
            chip_out[slot, place, 0] = up_block.astype(BF16)
            chip_out[slot, place, 1] = down_block.astype(BF16)
        for copy in to_chips(slot):
            copy.start()

    @pl.when((step >= 2) & (step < tiles + 2))
    def _():
        slot = lax.rem(step, 2)
        for copy in to_seq(slot):
            copy.wait()
        up_quarter[slot] = up_half[slot, y] + up_got[slot, y].astype(F32)
        up_last[slot] = (up_half[slot, 1 - y] + up_got[slot, 1 - y].astype(F32)).astype(BF16)
        down_quarter[slot] = down_half[slot, x] + down_got[slot, x].astype(F32)
        down_last[slot] = (down_half[slot, 1 - x] + down_got[slot, 1 - x].astype(F32)).astype(BF16)
        for copy in to_last(slot):
            copy.start()

    @pl.when((step >= 1) & (step <= tiles))
    def _():
        slot = lax.rem(step + 1, 2)
        for copy in to_core(slot):
            copy.wait()
        for other in range(2):
            kept, gone = 2 * other + x, 2 * other + 1 - x
            up_half[slot, other] = up_mine[slot, kept] + up_core_got[slot, kept].astype(F32)
            up_out[slot, other] = (up_mine[slot, gone] + up_core_got[slot, gone].astype(F32)).astype(BF16)
            kept, gone = 2 * y + other, 2 * (1 - y) + other
            down_half[slot, other] = down_mine[slot, kept] + down_core_got[slot, kept].astype(F32)
            down_out[slot, other] = (down_mine[slot, gone] + down_core_got[slot, gone].astype(F32)).astype(BF16)
        for copy in to_seq(slot):
            copy.start()

    @pl.when(step < tiles)
    def _():
        slot = lax.rem(step, 2)
        up = jnp.concatenate([up0[...], up1[...], up2[...], up3[...]], axis=1)
        down = jnp.concatenate([down0[...], down1[...], down2[...], down3[...]], axis=0)
        biases = jnp.concatenate([bias[owner] for owner in range(4)], axis=1)
        c0 = math.sqrt(2 / math.pi)
        c1 = c0 * 0.044715
        hidden = jnp.dot(normed[...], up, preferred_element_type=F32) + biases
        square = hidden * hidden
        gate = 0.5 + 0.5 * jnp.tanh(hidden * (c0 + c1 * square))
        raised = hidden * gate
        slope = gate + raised * (1.0 - gate) * (2 * c0 + 6 * c1 * square)
        active = raised.astype(BF16)
        down_part = jnp.dot(grad_turned[...], active, preferred_element_type=F32)
        for owner in range(4):
            size = half // 4
            down_mine[slot, owner] = down_part[owner * size : (owner + 1) * size]
            down_core[slot, owner] = down_part[half + owner * size : half + (owner + 1) * size].astype(BF16)
        to_core(slot)[1].start()
        back = (((1,), (1,)), ((), ()))
        grad_active = lax.dot_general(grad_out[...], down, back, preferred_element_type=F32)
        grad_wide = (grad_active * slope).astype(BF16)
        up_part = jnp.dot(normed_turned[...], grad_wide, preferred_element_type=F32)
        for owner in range(4):
            columns = slice(owner * 128, (owner + 1) * 128)
            up_mine[slot, owner] = up_part[:half, columns]
            up_core[slot, owner] = up_part[half:, columns].astype(BF16)
        to_core(slot)[0].start()
        sums = jnp.sum(grad_wide.astype(F32), axis=0, keepdims=True)
        for owner in range(4):
            bias_sum[owner] = sums[:, owner * 128 : (owner + 1) * 128]
        out_part = jnp.dot(active, down, preferred_element_type=F32)
        grad_part = lax.dot_general(grad_wide, up, back, preferred_element_type=F32)

        @pl.when(step == 0)
        def _():
            out_sum[...] = out_part
            grad_sum[...] = grad_part

        @pl.when(step > 0)
        def _():
            out_sum[...] += out_part
            grad_sum[...] += grad_part


def feed_forward_reduce(normed, grad_out, normed_turned, grad_turned, up, down, bias):
    count, width = normed.shape
    hidden = up.shape[1]
    part = hidden // 4
    tiles = part // 128
    half, quarter = width // 2, width // 8
    last = tiles - 1
    shape = jax.ShapeDtypeStruct
    fixed = lambda *dims: pl.BlockSpec(dims, lambda t: (0, 0), pipeline_mode=pl.Buffered(buffer_count=1))
    result = lambda *dims: pl.BlockSpec(dims, lambda t: (0, 0))
    done = lambda t: jnp.maximum(t - STAGES, 0)

    def up_block(owner):
        return pl.BlockSpec((width, 128), lambda t: (0, owner * tiles + jnp.minimum(t, last)))

    def down_block(owner):
        return pl.BlockSpec((128, width), lambda t: (owner * tiles + jnp.minimum(t, last), 0))

    bias_block = pl.BlockSpec((4, 1, 128), lambda t: (0, 0, jnp.minimum(t, last)))
    pair = lambda dtype, *dims: pltpu.VMEM((2,) + dims, dtype)
    return pl.pallas_call(
        partial(mlp_reduce_kernel, tiles),
        grid=(tiles + STAGES,),
        in_specs=[fixed(count, width), fixed(count, width), fixed(width, count), fixed(width, count)]
        + [up_block(owner) for owner in range(4)]
        + [down_block(owner) for owner in range(4)]
        + [bias_block],
        out_specs=[
            result(count, width),
            result(count, width),
            bias_block,
            pl.BlockSpec((quarter, 128), lambda t: (0, done(t))),
            pl.BlockSpec((quarter, 128), lambda t: (0, done(t))),
        ],
        out_shape=[
            shape((count, width), F32),
            shape((count, width), F32),
            shape((4, 1, part), F32),
            shape((quarter, part), F32),
            shape((quarter, part), F32),
        ],
        scratch_shapes=[
            pair(F32, 4, half, 128),
            pair(F32, 4, quarter, 512),
            pair(BF16, 4, half, 128),
            pair(BF16, 4, quarter, 512),
            pair(BF16, 4, half, 128),
            pair(BF16, 4, quarter, 512),
            pair(F32, 2, half, 128),
            pair(F32, 2, quarter, 512),
            pair(BF16, 2, half, 128),
            pair(BF16, 2, quarter, 512),
            pair(BF16, 2, half, 128),
            pair(BF16, 2, quarter, 512),
            pair(F32, half, 128),
            pair(F32, quarter, 512),
            pair(BF16, half, 128),
            pair(BF16, quarter, 512),
            pair(BF16, half, 128),
            pair(BF16, quarter, 512),
            pair(F32, 4, 2, quarter, 128),
            pair(BF16, 4, 2, quarter, 128),
            pair(BF16, 3, 2, quarter, 128),
        ]
        + [pltpu.SemaphoreType.DMA((2, 2))] * 6
        + [pltpu.SemaphoreType.DMA((3, 2))] * 2,
        compiler_params=pltpu.CompilerParams(collective_id=1, has_side_effects=True, vmem_limit_bytes=VMEM_LIMIT),
        cost_estimate=pl.CostEstimate(
            flops=12 * count * width * hidden,
            bytes_accessed=6 * width * hidden,
            transcendentals=count * hidden,
        ),
    )(normed, grad_out, normed_turned, grad_turned, up, up, up, up, down, down, down, down, bias.reshape(4, 1, part))


def split_low(values):
    high = values.astype(BF16)
    rest = values - high.astype(F32)
    middle = rest.astype(BF16)
    return high, middle, (rest - middle.astype(F32)).astype(BF16)


def per_token(slot_col, seg_row, table):
    picked = (slot_col == seg_row).astype(BF16)
    return lax.dot_general(
        picked, jnp.concatenate(split_low(table), axis=0), (((0,), (0,)), ((), ())), preferred_element_type=F32
    )


def per_slot(slot_col, seg_row, values):
    slots = slot_col.shape[0] // 3
    picked = (slot_col[:slots] == seg_row).astype(BF16)
    return sum(jnp.dot(picked, part, preferred_element_type=F32) for part in split_low(values))


def normalize(values):
    center = values - jnp.mean(values, axis=-1, keepdims=True)
    inverse = lax.rsqrt(jnp.mean(center * center, axis=-1, keepdims=True) + norm_eps)
    return center * inverse, inverse


def normalize_back(normal, inverse, grad):
    return inverse * (grad - jnp.mean(grad, axis=-1, keepdims=True) - normal * jnp.mean(grad * normal, axis=-1, keepdims=True))


def after_kernel(
    slot_col,
    seg,
    table,
    attended,
    weight,
    bias,
    out_sum,
    grad_sum,
    middle_ref,
    branch_ref,
    cotangent,
    block_out,
    grad_middle_ref,
    slot_sums,
    bias_sum,
    view_ref,
    proj_ref,
    heads_out,
    total,
    core_out,
    core_got,
    sent,
    came,
    kept,
    core_sent,
    core_came,
):
    step = pl.program_id(0)
    rows = pl.num_programs(0)
    width = cotangent.shape[-1]
    length = cotangent.shape[-2]
    depth, own = width // 8, width // 4
    seq, row = lax.axis_index("seq"), lax.axis_index("rows")
    core = lax.rem(row, 2)
    core_peer = {"rows": row + 1 - 2 * core}
    peers = peers_of(seq)

    @pl.when(step == 0)
    def _():
        greet([{"seq": peer} for peer in peers] + [core_peer])

    def to_peer(r, m):
        lanes = pl.ds(m * length, length)
        return send_block(
            heads_out.at[r, peers[m - 1]], view_ref.at[r, :, lanes], sent, came, r * 3 + m - 1, {"seq": peers[m - 1]}
        )

    def to_self(r):
        return pltpu.make_async_copy(heads_out.at[r, seq], view_ref.at[r, :, pl.ds(0, length)], kept.at[r])

    mods = per_token(slot_col[...], seg[0], table[0, :, 2 * width :])
    gate_a, scale_b, gate_b = (mods[:, k * width : (k + 1) * width] for k in (0, 2, 3))
    middle, branch = middle_ref[0], branch_ref[0]
    upstream = cotangent[0].astype(F32)
    normal, inverse = normalize(middle)
    grad_normed = grad_sum[...]
    grad_middle = upstream + normalize_back(normal, inverse, grad_normed * (1.0 + scale_b))
    grad_middle_ref[0] = grad_middle
    grad_branch = (grad_middle * gate_a).astype(BF16)
    grad_heads = lax.dot_general(weight[...], grad_branch, (((1,), (1,)), ((), ())), preferred_element_type=F32)
    for owner in range(4):
        heads_out[step, owner] = grad_heads[owner * own : (owner + 1) * own].astype(BF16)
    to_self(step).start()
    for m in range(1, 4):
        to_peer(step, m).start()

    part = jnp.dot(attended[0], grad_branch, preferred_element_type=F32)
    sums = jnp.sum(grad_branch.astype(F32), axis=0, keepdims=True)

    @pl.when(step == 0)
    def _():
        total[...] = part
        bias_sum[...] = sums

    @pl.when(step > 0)
    def _():
        total[...] += part
        bias_sum[...] += sums

    to_core = pltpu.make_async_remote_copy(
        src_ref=core_out,
        dst_ref=core_got,
        send_sem=core_sent,
        recv_sem=core_came,
        device_id=core_peer,
        device_id_type=pl.DeviceIdType.MESH,
    )

    @pl.when(step == rows - 1)
    def _():
        for chip in range(4):
            other = pl.multiple_of((2 * chip + 1 - core) * depth, 8)
            core_out[chip] = total[pl.ds(other, depth), :].astype(BF16)
        to_core.start()

    branch_b = out_sum[...] + bias[...]
    block_out[0] = (middle + gate_b * branch_b).astype(BF16)
    pieces = (grad_middle * branch, grad_normed, grad_normed * normal, upstream * branch_b)
    for k, piece in enumerate(pieces):
        slot_sums[0, :, k * width : (k + 1) * width] = per_slot(slot_col[...], seg[0], piece)

    @pl.when(step == rows - 1)
    def _():
        to_core.wait()
        for chip in range(4):
            mine = pl.multiple_of((2 * chip + core) * depth, 8)
            proj_ref[chip] = total[pl.ds(mine, depth), :] + core_got[chip].astype(F32)
        for r in range(heads_out.shape[0]):
            to_self(r).wait()
            for m in range(1, 4):
                to_peer(r, m).wait()


def after_feed_forward(slot_col, seg, table, attended, weight, bias, out_sum, grad_sum, middle, branch, cotangent):
    rows, length, width = cotangent.shape
    slots = table.shape[1]
    depth = width // 8
    fixed = lambda *dims: pl.BlockSpec(dims, lambda r: (0,) * len(dims))
    row = lambda *dims: pl.BlockSpec((1,) + dims, lambda r: (r, 0, 0))
    shape = jax.ShapeDtypeStruct
    return pl.pallas_call(
        after_kernel,
        grid=(rows,),
        in_specs=[
            fixed(*slot_col.shape),
            row(1, length),
            row(*table.shape[1:]),
            row(width, length),
            fixed(width, width),
            fixed(1, width),
            pl.BlockSpec((length, width), lambda r: (r, 0)),
            pl.BlockSpec((length, width), lambda r: (r, 0)),
            row(length, width),
            row(length, width),
            row(length, width),
        ],
        out_specs=[
            row(length, width),
            row(length, width),
            row(slots, 4 * width),
            fixed(1, width),
            pl.BlockSpec(memory_space=pl.ANY),
            fixed(4, depth, width),
        ],
        out_shape=[
            shape((rows, length, width), BF16),
            shape((rows, length, width), F32),
            shape((rows, slots, 4 * width), F32),
            shape((1, width), F32),
            shape((rows, width // 4, 4 * length), BF16),
            shape((4, depth, width), F32),
        ],
        scratch_shapes=[
            pltpu.VMEM((rows, 4, width // 4, length), BF16),
            pltpu.VMEM((width, width), F32),
            pltpu.VMEM((4, depth, width), BF16),
            pltpu.VMEM((4, depth, width), BF16),
            pltpu.SemaphoreType.DMA((3 * rows,)),
            pltpu.SemaphoreType.DMA((3 * rows,)),
            pltpu.SemaphoreType.DMA((rows,)),
            pltpu.SemaphoreType.DMA,
            pltpu.SemaphoreType.DMA,
        ],
        compiler_params=pltpu.CompilerParams(vmem_limit_bytes=VMEM_LIMIT, collective_id=4, has_side_effects=True),
        cost_estimate=pl.CostEstimate(flops=8 * 10**9, bytes_accessed=3 * 10**7, transcendentals=0),
    )(slot_col, seg, table, attended, weight, bias, out_sum, grad_sum, middle, branch, cotangent)


def qkv_weight_kernel(grad, normed, keep_ref, send_ref, sum_ref, total, turned):
    step = pl.program_id(0)
    chips, depth = lax.axis_size("rows") // 2, total.shape[1] // lax.axis_size("rows")
    mine = lax.rem(lax.axis_index("rows"), 2)
    part = jnp.dot(grad[0], normed[0], preferred_element_type=F32)
    sums = jnp.sum(grad[0].astype(F32), axis=1, keepdims=True)

    @pl.when(step == 0)
    def _():
        total[...] = part
        sum_ref[...] = sums

    @pl.when(step > 0)
    def _():
        total[...] += part
        sum_ref[...] += sums

    @pl.when(step == pl.num_programs(0) - 1)
    def _():
        turned[...] = total[...].T
        for chip in range(chips):
            first = pl.multiple_of((2 * chip + mine) * depth, 8)
            other = pl.multiple_of((2 * chip + 1 - mine) * depth, 8)
            keep_ref[chip] = turned[pl.ds(first, depth), :]
            send_ref[chip] = turned[pl.ds(other, depth), :].astype(BF16)


def qkv_weight_grad(grad, normed):
    rows, features, length = grad.shape
    width = normed.shape[2]
    groups = lax.axis_size("rows")
    shape = (groups // 2, width // groups, features)
    return pl.pallas_call(
        qkv_weight_kernel,
        grid=(rows,),
        in_specs=[
            pl.BlockSpec((1, features, length), lambda r: (r, 0, 0)),
            pl.BlockSpec((1, length, width), lambda r: (r, 0, 0)),
        ],
        out_specs=[
            pl.BlockSpec(shape, lambda r: (0, 0, 0)),
            pl.BlockSpec(shape, lambda r: (0, 0, 0)),
            pl.BlockSpec((features, 1), lambda r: (0, 0)),
        ],
        out_shape=[
            jax.ShapeDtypeStruct(shape, F32),
            jax.ShapeDtypeStruct(shape, BF16),
            jax.ShapeDtypeStruct((features, 1), F32),
        ],
        scratch_shapes=[pltpu.VMEM((features, width), F32), pltpu.VMEM((width, features), F32)],
        compiler_params=pltpu.CompilerParams(vmem_limit_bytes=VMEM_LIMIT),
        cost_estimate=pl.CostEstimate(
            flops=2 * rows * length * width * features,
            bytes_accessed=2 * rows * length * (width + features) + 6 * width * features // 2,
            transcendentals=0,
        ),
    )(grad, normed)


def tail_kernel(
    images,
    mod,
    weight,
    cond,
    ada_ref,
    cond_ref,
    bias_ref,
    got,
    low_mine,
    low_got,
    row_mine,
    row_got,
    cond_mine,
    cond_got,
    column_got,
    sent,
    arrived,
):
    seq_count, row_total = lax.axis_size("seq"), lax.axis_size("rows")
    seq, row = lax.axis_index("seq"), lax.axis_index("rows")
    to_seq = [lax.rem(seq + m, seq_count) for m in range(seq_count)]
    to_row = [lax.rem(row + m, row_total) for m in range(row_total)]
    barrier = pltpu.get_barrier_semaphore()
    for m in range(1, seq_count):
        pl.semaphore_signal(barrier, inc=1, device_id={"seq": to_seq[m]}, device_id_type=pl.DeviceIdType.MESH)
    for m in range(1, row_total):
        pl.semaphore_signal(barrier, inc=1, device_id={"rows": to_row[m]}, device_id_type=pl.DeviceIdType.MESH)
    pl.semaphore_wait(barrier, seq_count + row_total - 2)

    used = [0]

    def start(source, target, device):
        copy = pltpu.make_async_remote_copy(
            src_ref=source,
            dst_ref=target,
            send_sem=sent.at[used[0]],
            recv_sem=arrived.at[used[0]],
            device_id=device,
            device_id_type=pl.DeviceIdType.MESH,
        )
        used[0] += 1
        copy.start()
        return copy

    copies = [start(mod.at[to_seq[m]], got.at[m], {"seq": to_seq[m]}) for m in range(1, seq_count)]
    column_got[0] = cond[row]
    column_copies = [start(cond.at[to_row[m]], column_got.at[m], {"rows": to_row[m]}) for m in range(1, row_total)]
    total = mod[seq]
    for m, copy in enumerate(copies):
        copy.wait()
        total = total + got[m + 1]
    low = total[:images].astype(BF16)
    low_mine[...] = low
    row_mine[...] = total[images:]
    row_mine[0:1] = jnp.sum(total[:images], axis=0, keepdims=True)
    low_got[0] = low
    copies = [start(low_mine, low_got.at[m], {"rows": to_row[m]}) for m in range(1, row_total)]
    copies += [start(row_mine, row_got.at[m], {"rows": to_row[m]}) for m in range(1, row_total)]
    term = lax.dot_general(low, weight[...], (((1,), (1,)), ((), ())), preferred_element_type=F32)
    cond_mine[...] = term
    cond_copies = [start(cond_mine, cond_got.at[m], {"seq": to_seq[m]}) for m in range(1, seq_count)]
    for copy in copies:
        copy.wait()
    sums = row_mine[...]
    for m in range(1, row_total):
        sums = sums + row_got[m]
    bias_ref[seq] = sums
    copies = [start(bias_ref.at[seq], bias_ref.at[seq], {"seq": to_seq[m]}) for m in range(1, seq_count)]
    for copy in column_copies:
        copy.wait()
    gathered = jnp.concatenate([low_got[m] for m in range(row_total)], axis=0)
    columns = jnp.concatenate([column_got[m] for m in range(row_total)], axis=0)
    ada_ref[...] = lax.dot_general(columns, gathered, (((0,), (0,)), ((), ())), preferred_element_type=F32)
    for m, copy in enumerate(cond_copies):
        copy.wait()
        term = term + cond_got[m + 1]
    cond_ref[...] = term
    for copy in copies:
        copy.wait()


def finish(mod, weight, cond, images):
    seq_count, lines, columns = mod.shape
    width, depth = weight.shape[0], cond.shape[2]
    row_total = lax.axis_size("rows")
    extra = lines - images
    copies = 3 * (seq_count - 1) + 3 * (row_total - 1)
    return pl.pallas_call(
        partial(tail_kernel, images),
        in_specs=[pl.BlockSpec(memory_space=pltpu.VMEM)] * 3,
        out_specs=[pl.BlockSpec(memory_space=pltpu.VMEM)] * 3,
        out_shape=[
            jax.ShapeDtypeStruct((depth, columns), F32),
            jax.ShapeDtypeStruct((images, width), F32),
            jax.ShapeDtypeStruct((seq_count, extra, columns), F32),
        ],
        scratch_shapes=[
            pltpu.VMEM((seq_count, lines, columns), F32),
            pltpu.VMEM((images, columns), BF16),
            pltpu.VMEM((row_total, images, columns), BF16),
            pltpu.VMEM((extra, columns), F32),
            pltpu.VMEM((row_total, extra, columns), F32),
            pltpu.VMEM((images, width), F32),
            pltpu.VMEM((seq_count, images, width), F32),
            pltpu.VMEM((row_total, images, depth), BF16),
            pltpu.SemaphoreType.DMA((copies,)),
            pltpu.SemaphoreType.DMA((copies,)),
        ],
        compiler_params=pltpu.CompilerParams(collective_id=0, has_side_effects=True, vmem_limit_bytes=VMEM_LIMIT),
        cost_estimate=pl.CostEstimate(flops=10**9, bytes_accessed=10**7, transcendentals=0),
    )(mod, weight, cond)


def send_to(source, target, sent, came, device):
    return pltpu.make_async_remote_copy(
        src_ref=source,
        dst_ref=target,
        send_sem=sent,
        recv_sem=came,
        device_id=device,
        device_id_type=pl.DeviceIdType.MESH,
    )


def attend_back_reduce_kernel(
    block,
    inner,
    scale,
    code_col,
    code_row,
    query,
    key,
    value,
    out,
    grad_out,
    lse,
    normed,
    proj,
    down,
    token_ref,
    qkv_ref,
    proj_ref,
    down_ref,
    grads,
    key_sum,
    value_sum,
    keys,
    values,
    flat,
    total,
    turned,
    core_out,
    core_got,
    proj_out,
    proj_got,
    seq_out,
    seq_got,
    down_out,
    down_got,
    sent,
    came,
    kept,
    proj_sent,
    proj_came,
    seq_sent,
    seq_came,
    core_sent,
    core_came,
):
    length, size = query.shape[-1], query.shape[-2]
    row, head = pl.program_id(0), pl.program_id(1)
    rows, _, heads = grads.shape[:3]
    width = normed.shape[-1]
    depth, own, local = width // 8, width // 4, length // 4
    seq, group = lax.axis_index("seq"), lax.axis_index("rows")
    chip, core = lax.div(group, 2), lax.rem(group, 2)
    peers = [{"seq": peer} for peer in peers_of(seq)]
    core_peer = {"rows": group + 1 - 2 * core}
    to_chip = [lax.rem(chip + k, 4) for k in range(4)]
    chip_peers = [{"rows": 2 * to_chip[k] + core} for k in range(4)]
    first = (row == 0) & (head == 0)
    last = (row == rows - 1) & (head == heads - 1)

    def to_peer(r, h, m):
        place = (r * heads + h) * 3 + m - 1
        source = grads.at[r, :, h, :, pl.ds(m * local, local)]
        return send_to(source, token_ref.at[r, :, seq, h], sent.at[place], came.at[place], peers[m - 1])

    def to_self(r, h):
        source = grads.at[r, :, h, :, pl.ds(0, local)]
        return pltpu.make_async_copy(source, token_ref.at[r, :, seq, h], kept.at[r * heads + h])

    proj_copies = [
        send_to(proj_out.at[to_chip[k]], proj_got.at[k - 1], proj_sent.at[k - 1], proj_came.at[k - 1], chip_peers[k])
        for k in range(1, 4)
    ]
    seq_copies = [
        send_to(seq_out.at[target], seq_got.at[m], seq_sent.at[m], seq_came.at[m], peers[m])
        for m, target in enumerate(peers_of(seq))
    ]
    core_copy = send_to(core_out, core_got, core_sent.at[0], core_came.at[0], core_peer)
    down_copy = send_to(down_out.at[1 - core], down_got, core_sent.at[1], core_came.at[1], core_peer)

    @pl.when(first)
    def _():
        greet(peers + [core_peer] + chip_peers[1:])
        proj_out[...] = proj[...].astype(BF16)
        for copy in proj_copies:
            copy.start()
        half = down.shape[1] // 2
        for place in range(2):
            down_out[place] = down[:, place * half : (place + 1) * half]
        down_copy.start()

    keys[...] = key[0, 0].astype(F32).T.astype(BF16)
    values[...] = value[0, 0].astype(F32).T.astype(BF16)

    def place_of(part):
        return pl.ds(pl.multiple_of((part * heads + head) * size, 8), size)

    for step in range(length // block):
        here = pl.ds(step * block, block)
        query_low = query[0, 0, :, here]
        grad_low = grad_out[0, 0, :, here]
        query_rows = query_low.astype(F32).T.astype(BF16)
        grad_rows = grad_low.astype(F32).T.astype(BF16)
        row_dot = jnp.sum(grad_low.astype(F32) * out[0, 0, :, here].astype(F32), axis=0, keepdims=True)
        grad_query = jnp.zeros((size, block), F32)
        for part in range(length // inner):
            there = pl.ds(part * inner, inner)
            scores = jnp.dot(keys[there, :], query_low, preferred_element_type=F32)
            scores = jnp.where(code_col[0, there, :] == code_row[0, :, here], scores * (scale * LOG2E), -1e30)
            probs = jnp.exp2(scores - lse[0, 0, :, here])
            grad_probs = jnp.dot(values[there, :], grad_low, preferred_element_type=F32)
            grad_raw = (probs * (grad_probs - row_dot) * scale).astype(BF16)
            value_part = jnp.dot(probs.astype(BF16), grad_rows, preferred_element_type=F32)
            key_part = jnp.dot(grad_raw, query_rows, preferred_element_type=F32)
            if step == 0:
                value_sum[there, :] = value_part
                key_sum[there, :] = key_part
            else:
                value_sum[there, :] += value_part
                key_sum[there, :] += key_part
            grad_query += jnp.dot(key[0, 0, :, there], grad_raw, preferred_element_type=F32)
        low = grad_query.astype(BF16)
        grads[row, 0, head, :, here] = low
        flat[place_of(0), here] = low.astype(F32)
    for part, sums in ((1, key_sum), (2, value_sum)):
        low = sums[...].T.astype(BF16)
        grads[row, part, head] = low
        flat[place_of(part), :] = low.astype(F32)

    to_self(row, head).start()
    for m in range(1, 4):
        to_peer(row, head, m).start()

    @pl.when((head == heads - 1) & (row == 0))
    def _():
        total[...] = jnp.dot(flat[...].astype(BF16), normed[0], preferred_element_type=F32)

    @pl.when((head == heads - 1) & (row > 0))
    def _():
        total[...] += jnp.dot(flat[...].astype(BF16), normed[0], preferred_element_type=F32)

    @pl.when(last)
    def _():
        turned[...] = total[...].T
        for place in range(4):
            other = pl.multiple_of((2 * place + 1 - core) * depth, 8)
            core_out[place] = turned[pl.ds(other, depth), :].astype(BF16)
        core_copy.start()
        for copy in proj_copies:
            copy.wait()
        mine = proj[chip]
        for k in range(3):
            mine = mine + proj_got[k].astype(F32)
        for place in range(4):
            seq_out[place] = mine[:, place * own : (place + 1) * own].astype(BF16)
        for copy in seq_copies:
            copy.start()
        down_copy.wait()
        left, right = down_out[core], down_got[...]
        left, right = jnp.where(core == 0, left, right), jnp.where(core == 0, right, left)
        down_ref[:depth] = left
        down_ref[depth:] = right
        core_copy.wait()
        for place in range(4):
            same = pl.multiple_of((2 * place + core) * depth, 8)
            qkv_ref[place] = turned[pl.ds(same, depth), :] + core_got[place].astype(F32)
        for place in range(4):

            @pl.when(seq == place)
            def _():
                proj_ref[...] = mine[:, place * own : (place + 1) * own]

        for m, copy in enumerate(seq_copies):
            copy.wait()
            proj_ref[...] += seq_got[m].astype(F32)
        for r in range(rows):
            for h in range(heads):
                to_self(r, h).wait()
                for m in range(1, 4):
                    to_peer(r, h, m).wait()


def attend_back_reduce(packed, out, grad_out, lse, col, row, normed, proj, down, block, inner):
    rows, _, heads, size, length = packed.shape
    width = normed.shape[2]
    depth, own, features = width // 8, width // 4, 3 * heads * size
    half = down.shape[1] // 2
    part = lambda j: pl.BlockSpec((1, None, 1, size, length), lambda r, h: (r, j, h, 0, 0))
    whole = pl.BlockSpec((1, 1, size, length), lambda r, h: (r, h, 0, 0))
    fixed = lambda *dims: pl.BlockSpec(dims, lambda r, h: (0,) * len(dims))
    shape = jax.ShapeDtypeStruct
    count = rows * heads
    dma = lambda n: pltpu.SemaphoreType.DMA((n,))
    return pl.pallas_call(
        partial(attend_back_reduce_kernel, block, inner, size**-0.5),
        grid=(rows, heads),
        in_specs=[
            pl.BlockSpec((1, length, 1), lambda r, h: (r, 0, 0)),
            pl.BlockSpec((1, 1, length), lambda r, h: (r, 0, 0)),
            part(0),
            part(1),
            part(2),
            whole,
            whole,
            pl.BlockSpec((1, 1, 1, length), lambda r, h: (r, h, 0, 0)),
            pl.BlockSpec((1, length, width), lambda r, h: (r, 0, 0)),
            fixed(4, depth, width),
            fixed(depth, 2 * half),
        ],
        out_specs=[pl.BlockSpec(memory_space=pl.ANY), fixed(4, depth, features), fixed(depth, own), fixed(own, half)],
        out_shape=[
            shape((rows, 3, 4, heads, size, length // 4), BF16),
            shape((4, depth, features), F32),
            shape((depth, own), F32),
            shape((own, half), F32),
        ],
        scratch_shapes=[
            pltpu.VMEM((rows, 3, heads, size, length), BF16),
            pltpu.VMEM((length, size), F32),
            pltpu.VMEM((length, size), F32),
            pltpu.VMEM((length, size), BF16),
            pltpu.VMEM((length, size), BF16),
            pltpu.VMEM((features, length), F32),
            pltpu.VMEM((features, width), F32),
            pltpu.VMEM((width, features), F32),
            pltpu.VMEM((4, depth, features), BF16),
            pltpu.VMEM((4, depth, features), BF16),
            pltpu.VMEM((4, depth, width), BF16),
            pltpu.VMEM((3, depth, width), BF16),
            pltpu.VMEM((4, depth, own), BF16),
            pltpu.VMEM((3, depth, own), BF16),
            pltpu.VMEM((2, depth, half), F32),
            pltpu.VMEM((depth, half), F32),
            dma(3 * count),
            dma(3 * count),
            dma(count),
            dma(3),
            dma(3),
            dma(3),
            dma(3),
            dma(2),
            dma(2),
        ],
        compiler_params=pltpu.CompilerParams(vmem_limit_bytes=VMEM_LIMIT, collective_id=3, has_side_effects=True),
        cost_estimate=pl.CostEstimate(
            flops=20 * rows * heads * length * length * 128,
            bytes_accessed=16 * rows * heads * length * size,
            transcendentals=rows * heads * length * length,
        ),
    )(col, row, packed, packed, packed, out, grad_out, lse, normed, proj, down)


def last_kernel(
    slot_col,
    seg,
    table,
    grads,
    weight,
    tokens,
    grad_middle,
    slot_sums,
    pick,
    conditioning,
    biases,
    qkv,
    cond,
    ada,
    grad_tokens,
    ada_ref,
    cond_ref,
    ada_bias_ref,
    qv_bias_ref,
    proj_bias_ref,
    up_bias_ref,
    down_bias_ref,
    qkv_ref,
    ada_here,
    image_sums,
    feature_sums,
    mod,
    got,
    lines,
    lines_got,
    low_all,
    small_core,
    small_chip,
    small_seq,
    cond_all,
    column_got,
    chip_out,
    chip_got,
    piece_out,
    piece_got,
    ada_came,
    sent,
    came,
):
    step, rows = pl.program_id(0), pl.num_programs(0)
    seq, group = lax.axis_index("seq"), lax.axis_index("rows")
    width = tokens.shape[-1]
    images = image_sums.shape[0]
    columns = mod.shape[2]
    own = width // 4
    chip, core = lax.div(group, 2), lax.rem(group, 2)
    seq_peers = peers_of(seq)
    to_seq = [{"seq": peer} for peer in seq_peers]
    rows_peers = [lax.rem(group + m, 8) for m in range(8)]
    to_row = [{"rows": peer} for peer in rows_peers]
    chips = [lax.rem(chip + k, 4) for k in range(4)]
    load_ada = pltpu.make_async_copy(ada, ada_here, ada_came)
    used = [0]

    def copy_to(source, target, device):
        used[0] += 1
        return send_to(source, target, sent.at[used[0] - 1], came.at[used[0] - 1], device)

    chip_copies = [copy_to(chip_out.at[chips[k]], chip_got.at[k - 1], {"rows": 2 * chips[k] + core}) for k in range(1, 4)]
    column_copies = [copy_to(cond.at[rows_peers[m]], column_got.at[group], to_row[m]) for m in range(1, 8)]
    mod_copies = [copy_to(mod.at[seq_peers[m]], got.at[m], to_seq[m]) for m in range(3)]
    line_copies = [copy_to(lines.at[seq_peers[m]], lines_got.at[m], to_seq[m]) for m in range(3)]
    core_peer = {"rows": group + 1 - 2 * core}
    chip_peers = [{"rows": 2 * chips[k] + core} for k in range(4)]
    low_core = copy_to(low_all.at[chip, core], low_all.at[chip, core], core_peer)
    low_chips = [copy_to(low_all.at[chip, core], low_all.at[chip, core], chip_peers[k]) for k in range(1, 4)]
    before = [lax.rem(chip + 4 - k, 4) for k in range(4)]
    low_on = [copy_to(low_all.at[before[k], core], low_all.at[before[k], core], core_peer) for k in range(1, 4)]
    small_over = copy_to(small_core.at[core], small_core.at[core], core_peer)
    small_chips = [copy_to(small_chip.at[chip], small_chip.at[chip], chip_peers[k]) for k in range(1, 4)]
    small_copies = [copy_to(small_seq.at[seq], small_seq.at[seq], to_seq[m]) for m in range(3)]
    cond_copies = [copy_to(cond_all.at[seq], cond_all.at[seq], to_seq[m]) for m in range(3)]
    base = used[0]

    @pl.when(step == 0)
    def _():
        load_ada.start()
        greet(to_seq + to_row[1:])
        chip_out[...] = qkv[...].astype(BF16)
        for copy in chip_copies + column_copies:
            copy.start()
        column_got[group] = cond[group]
        image_sums[...] = jnp.zeros_like(image_sums)
        feature_sums[...] = jnp.zeros_like(feature_sums)

    grad_low = grads[0]
    grad_normed = jnp.dot(weight[...], grad_low, preferred_element_type=F32).T
    ones = jnp.ones((8, grad_low.shape[1]), BF16)
    feature_sums[...] += lax.dot_general(ones, grad_low, (((1,), (1,)), ((), ())), preferred_element_type=F32)
    normal, inverse = normalize(tokens[0].astype(F32))
    scale_a = per_token(slot_col[...], seg[0], table[0, :, width : 2 * width])
    grad_tokens[0] = grad_middle[0] + normalize_back(normal, inverse, grad_normed * (1.0 + scale_a))
    late = [per_slot(slot_col[...], seg[0], piece) for piece in (grad_normed, grad_normed * normal)]
    slots = jnp.concatenate(late + [slot_sums[0]], axis=1)
    image_sums[...] += jnp.dot(pick[0], slots, precision=lax.Precision.HIGHEST, preferred_element_type=F32)

    @pl.when(step == rows - 1)
    def _():
        for place in range(4):
            mod[place] = image_sums[:, place * columns : (place + 1) * columns]
        lines[...] = jnp.zeros_like(lines)
        for line in range(8):
            value = biases[line : line + 1]
            if line < 2:
                value = feature_sums[0:1, 2 * line * width : (2 * line + 1) * width]
            lines[line // 2, line % 2 : line % 2 + 1, :width] = value
        for copy in mod_copies + line_copies:
            copy.start()
        total = mod[seq]
        for m, copy in enumerate(mod_copies):
            copy.wait()
            total = total + got[m]
        low = total.astype(BF16)
        low_all[chip, core] = low
        low_core.start()
        for copy in low_chips:
            copy.start()
        small = lines[seq]
        for m, copy in enumerate(line_copies):
            copy.wait()
            small = small + lines_got[m]
        small_core[core] = small
        small_core[core, 2:3] = jnp.sum(total, axis=0, keepdims=True)
        small_over.start()
        load_ada.wait()
        cond_all[seq] = jnp.dot(low, ada_here[...], preferred_element_type=F32)
        for copy in cond_copies:
            copy.start()
        for copy in chip_copies:
            copy.wait()
        for copy in column_copies:
            copy.wait()
        mine = qkv[chip]
        for k in range(3):
            mine = mine + chip_got[k].astype(F32)
        for part in range(3):
            piece_out[part] = mine[:, part * own : (part + 1) * own]

        def piece(part):
            index = part * 4 + seq
            target, place = lax.div(index, 3), lax.rem(index, 3)
            copy = send_to(piece_out.at[part], piece_got.at[place], sent.at[base + part], came.at[base + place], {"seq": target})
            return copy, target, place

        def arriving(place):
            source = lax.rem(3 * seq + place, 4)
            copy = send_to(piece_out.at[0], piece_got.at[place], sent.at[base], came.at[base + place], {"seq": source})
            return copy, source

        for part in range(3):
            copy, target, place = piece(part)

            @pl.when(target != seq)
            def _():
                copy.start()

            @pl.when(target == seq)
            def _():
                piece_got[place] = piece_out[part]

        small_over.wait()
        small_chip[chip] = small_core[0] + small_core[1]
        for copy in small_chips:
            copy.start()
        for came_in, going_on in zip(low_chips, low_on):
            came_in.wait()
            going_on.start()
        for copy in small_chips:
            copy.wait()
        small_seq[seq] = (small_chip[0] + small_chip[1]) + (small_chip[2] + small_chip[3])
        for copy in small_copies:
            copy.start()
        low_core.wait()
        for copy in low_on:
            copy.wait()
        gathered = jnp.concatenate([low_all[m // 2, m % 2] for m in range(8)], axis=0)
        blocks = jnp.concatenate([column_got[m] for m in range(8)], axis=0)
        ada_ref[...] = lax.dot_general(blocks, gathered, (((0,), (0,)), ((), ())), preferred_element_type=F32)
        for part in range(3):
            copy, target, place = piece(part)

            @pl.when(target != seq)
            def _():
                copy.wait_send()

        for place in range(3):
            copy, source = arriving(place)

            @pl.when(source != seq)
            def _():
                copy.wait_recv()

        for place in range(3):
            qkv_ref[:, place * own : (place + 1) * own] = piece_got[place]
        for copy in cond_copies:
            copy.wait()
        term = (cond_all[0] + cond_all[1]) + (cond_all[2] + cond_all[3])
        value = conditioning[...]
        gate = 1.0 / (1.0 + jnp.exp(-value))
        cond_ref[...] = term * gate * (1.0 + value * (1.0 - gate))
        for copy in small_copies:
            copy.wait()
        for place in range(4):
            ada_bias_ref[:, place * columns : (place + 1) * columns] = small_seq[place, 2:3]
        qv_bias_ref[...] = small_seq[0, 0:2, :width]
        proj_bias_ref[...] = small_seq[1, 0:1, :width]
        for line in range(3, 7):
            up_bias_ref[:, (line - 3) * width : (line - 2) * width] = small_seq[line // 2, line % 2 : line % 2 + 1, :width]
        down_bias_ref[...] = small_seq[3, 1:2, :width]


def finish_all(slot_col, seg, table, grads, weight, tokens, grad_middle, slot_sums, pick, conditioning, biases, qkv, cond, ada):
    rows, length, width = tokens.shape
    images, columns = conditioning.shape[0], ada.shape[0]
    depth, own = width // 8, width // 4
    fixed = lambda *dims: pl.BlockSpec(dims, lambda r: (0,) * len(dims), pipeline_mode=pl.Buffered(buffer_count=1))
    result = lambda *dims: pl.BlockSpec(dims, lambda r: (0,) * len(dims))
    row = lambda *dims: pl.BlockSpec((1,) + dims, lambda r: (r, 0, 0))
    shape = jax.ShapeDtypeStruct
    vmem = lambda dtype, *dims: pltpu.VMEM(dims, dtype)
    copies = 3 + 7 + 3 + 3 + 1 + 3 + 3 + 1 + 3 + 3 + 3 + 3
    return pl.pallas_call(
        last_kernel,
        grid=(rows,),
        in_specs=[
            fixed(*slot_col.shape),
            row(1, length),
            row(*table.shape[1:]),
            row(3 * width, length),
            fixed(width, 3 * width),
            row(length, width),
            row(length, width),
            row(*slot_sums.shape[1:]),
            row(*pick.shape[1:]),
            fixed(images, width),
            fixed(8, width),
            fixed(4, depth, 3 * own),
            fixed(8, images, depth),
            pl.BlockSpec(memory_space=pl.ANY),
        ],
        out_specs=[
            row(length, width),
            result(depth, columns),
            result(images, width),
            result(1, 4 * columns),
            result(2, width),
            result(1, width),
            result(1, 4 * width),
            result(1, width),
            result(depth, 3 * own),
        ],
        out_shape=[
            shape((rows, length, width), F32),
            shape((depth, columns), F32),
            shape((images, width), F32),
            shape((1, 4 * columns), F32),
            shape((2, width), F32),
            shape((1, width), F32),
            shape((1, 4 * width), F32),
            shape((1, width), F32),
            shape((depth, 3 * own), F32),
        ],
        scratch_shapes=[
            vmem(BF16, columns, width),
            vmem(F32, images, 6 * width),
            vmem(F32, 8, 3 * width),
            vmem(F32, 4, images, columns),
            vmem(F32, 3, images, columns),
            vmem(F32, 4, 8, columns),
            vmem(F32, 3, 8, columns),
            vmem(BF16, 4, 2, images, columns),
            vmem(F32, 2, 8, columns),
            vmem(F32, 4, 8, columns),
            vmem(F32, 4, 8, columns),
            vmem(F32, 4, images, width),
            vmem(BF16, 8, images, depth),
            vmem(BF16, 4, depth, 3 * own),
            vmem(BF16, 3, depth, 3 * own),
            vmem(F32, 3, depth, own),
            vmem(F32, 3, depth, own),
            pltpu.SemaphoreType.DMA,
            pltpu.SemaphoreType.DMA((copies,)),
            pltpu.SemaphoreType.DMA((copies,)),
        ],
        compiler_params=pltpu.CompilerParams(vmem_limit_bytes=VMEM_LIMIT, collective_id=5, has_side_effects=True),
        cost_estimate=pl.CostEstimate(flops=5 * 10**9, bytes_accessed=3 * 10**7, transcendentals=0),
    )(slot_col, seg, table, grads, weight, tokens, grad_middle, slot_sums, pick, conditioning, biases, qkv, cond, ada)


def forward_kernel(
    block,
    slot_col,
    image_col,
    seg,
    fill,
    conditioning,
    ada_bias,
    qv_bias,
    proj_bias,
    tokens,
    ada,
    weight,
    proj,
    cotangent,
    normed_ref,
    packed_ref,
    attended_ref,
    features_ref,
    branch_ref,
    middle_ref,
    inner_ref,
    grad_ref,
    inner_turned_ref,
    grad_turned_ref,
    table_ref,
    code_row,
    code_col,
    lse_ref,
    bias_sum,
    here,
    normed_all,
    packed_all,
    ada_here,
    windows,
    turned,
    own_weight,
    bias_turned,
    mod_all,
    table,
    seg_all,
    attended_all,
    attended_got,
    flat,
    features_all,
    proj_here,
    cotangent_here,
    branch_all,
    middle_all,
    inner_all,
    grad_all,
    inner_turned,
    grad_turned,
    rows_turned,
    load_sem,
    own_sem,
    mod_sent,
    mod_came,
    sent,
    came,
    forward_sent,
    forward_came,
    heads_sent,
    heads_came,
    heads_kept,
    store_sem,
    last_sem,
):
    rows, _, local, width = here.shape
    _, parts, heads, size, length = packed_all.shape
    own, depth, half = heads * size, width // 8, local // 2
    columns = ada_here.shape[0]
    images, slots = conditioning.shape[0], image_col.shape[1]
    scale = size**-0.5 * LOG2E
    seq = lax.axis_index("seq")
    core = lax.rem(lax.axis_index("rows"), 2)
    places = [seq] + peers_of(seq)
    peers = [{"seq": place} for place in places]

    greet(peers[1:])

    def direct(r, m):
        index = r * 2 + m - 1
        return send_to(tokens.at[r], here.at[r, m], sent.at[index], came.at[index], peers[m])

    def forward(r, m):
        part = pl.ds(0, half) if m == 1 else pl.ds(half, half)
        index = r * 2 + m - 1
        return send_to(
            here.at[r, 3 - m, part], here.at[r, 3, part], forward_sent.at[index], forward_came.at[index], peers[m]
        )

    def go(copies):
        for copy in copies:
            copy.start()

    def end(copies):
        for copy in copies:
            copy.wait()

    go([direct(0, m) for m in (1, 2)])
    own_copies = [pltpu.make_async_copy(tokens.at[r], here.at[r, 0], own_sem.at[r]) for r in range(rows)]
    load_ada = pltpu.make_async_copy(ada, ada_here, load_sem.at[0])
    load_windows = []
    for part in range(3):
        lanes = pl.ds(pl.multiple_of(part * width + seq * 256, 128), 384)
        load_windows.append(pltpu.make_async_copy(weight.at[:, lanes], windows.at[part], load_sem.at[1 + part]))
    load_proj = pltpu.make_async_copy(proj, proj_here, load_sem.at[4])
    load_cotangent = pltpu.make_async_copy(cotangent, cotangent_here, load_sem.at[5])
    go([load_ada] + load_windows + own_copies + [load_proj, load_cotangent])

    value = conditioning[...].astype(F32)
    low = (value / (1.0 + jnp.exp(-value))).astype(BF16)
    load_ada.wait()
    mod_all[seq] = lax.dot_general(low, ada_here[...], (((1,), (1,)), ((), ())), preferred_element_type=F32)
    mod_copies = [
        send_to(mod_all.at[seq], mod_all.at[seq], mod_sent.at[m - 1], mod_came.at[m - 1], peers[m]) for m in range(1, 4)
    ]
    go(mod_copies)

    for m in range(4):
        lanes = pl.ds(pl.multiple_of(places[m] * local, 128), local)
        found = seg[:, lanes]
        where = places[m] * local + lax.broadcasted_iota(jnp.int32, (rows, local), 1)
        code = jnp.where(where < fill[...], found, -1 - where)
        for r in range(rows):
            seg_all[r, m] = found[r : r + 1]
            code_row[r, :, m * local : (m + 1) * local] = code[r : r + 1]
            column = jnp.broadcast_to(code[r : r + 1].astype(F32), (128, local)).T[:, :1]
            code_col[r, m * local : (m + 1) * local] = column.astype(jnp.int32)

    for part in range(3):
        load_windows[part].wait()
        turned[...] = windows[part].astype(F32).T
        own_weight[part * own : (part + 1) * own] = turned[pl.ds(pl.multiple_of(seq * 32, 8), own), :].astype(BF16)
    window = qv_bias[:, pl.ds(pl.multiple_of(seq * 256, 128), 384)].astype(F32)
    bias_turned[...] = jnp.concatenate([window, jnp.zeros((6, 384), F32)], axis=0).T
    bias = bias_turned[pl.ds(pl.multiple_of(seq * 32, 8), own), :]
    bias = jnp.concatenate([bias[:, 0:1], jnp.zeros((own, 1), F32), bias[:, 1:2]], axis=0)

    end([direct(0, m) for m in (1, 2)])
    go([forward(0, m) for m in (1, 2)] + [direct(1, m) for m in (1, 2)])

    end(mod_copies)
    for place in range(4):
        lanes = slice(place * columns, (place + 1) * columns)
        table[:, lanes] = mod_all[place] + ada_bias[:, lanes].astype(F32)
    stacked = jnp.concatenate(split_low(table[...]), axis=0)
    image_row = lax.rem(lax.broadcasted_iota(jnp.int32, (slots, 3 * images), 1), images)
    for r in range(rows):
        picked = (image_col[r] == image_row).astype(BF16)
        table_ref[r] = jnp.dot(picked, stacked, preferred_element_type=F32)

    def stores(r, m):
        index = r * 4 + m
        lanes = pl.ds(m * local, local)
        return (
            pltpu.make_async_copy(normed_all.at[r, m], normed_ref.at[r, m], store_sem.at[0, index]),
            pltpu.make_async_copy(packed_all.at[r, :, :, :, lanes], packed_ref.at[r, :, :, :, lanes], store_sem.at[1, index]),
        )

    def work(r, m):
        mods = per_token(slot_col[...], seg_all[r, m], table_ref[r, :, : 2 * width])
        normal, _ = normalize(here[r, m].astype(F32))
        normed = (normal * (1.0 + mods[:, width:]) + mods[:, :width]).astype(BF16)
        normed_all[r, m] = normed
        mixed = lax.dot_general(own_weight[...], normed, (((1,), (1,)), ((), ())), preferred_element_type=F32)
        mixed = (mixed + bias).astype(BF16)
        for part in range(parts):
            for head in range(heads):
                start = (part * heads + head) * size
                packed_all[r, part, head, :, m * local : (m + 1) * local] = mixed[start : start + size]
        go(stores(r, m))

    def to_peer(r, h, m):
        source = attended_all.at[r, h, :, pl.ds(m * local, local)]
        place = (r * heads + h) * 3 + m - 1
        return send_to(source, attended_got.at[r, seq, h], heads_sent.at[place], heads_came.at[place], peers[m])

    def to_self(r, h):
        source = attended_all.at[r, h, :, pl.ds(0, local)]
        return pltpu.make_async_copy(source, attended_got.at[r, seq, h], heads_kept.at[r * heads + h])

    def attend_head(r, h):
        keys = packed_all[r, 1, h].astype(F32).T.astype(BF16)
        values = packed_all[r, 2, h]
        codes = code_col[r]
        for step in range(length // block):
            lanes = pl.ds(step * block, block)
            scores = jnp.dot(keys, packed_all[r, 0, h, :, lanes], preferred_element_type=F32)
            scores = jnp.where(codes == code_row[r, :, lanes], scores * scale, -1e30)
            peak = jnp.max(scores, axis=0, keepdims=True)
            raised = jnp.exp2(scores - peak)
            total = jnp.sum(raised, axis=0, keepdims=True)
            probs = (raised * (1.0 / total)).astype(BF16)
            attended_all[r, h, :, lanes] = jnp.dot(values, probs, preferred_element_type=F32).astype(BF16)
            lse_ref[r, h, :, lanes] = peak + jnp.log2(total)
        to_self(r, h).start()
        for m in range(1, 4):
            to_peer(r, h, m).start()

    def attend_row(r, first, last):
        @pl.loop(first, last)
        def _(h):
            attend_head(r, h)

    end(own_copies)
    for m in range(3):
        work(0, m)
    end([forward(0, m) for m in (1, 2)])
    work(0, 3)
    attend_row(0, 0, heads // 2)
    end([direct(1, m) for m in (1, 2)])
    go([forward(1, m) for m in (1, 2)])
    attend_row(0, heads // 2, heads)
    for m in range(3):
        work(1, m)
    end([forward(1, m) for m in (1, 2)])
    work(1, 3)
    attend_row(1, 0, heads)
    end([load_proj, load_cotangent])

    def last_stores(r):
        lines, lanes = pl.ds(r * local, local), pl.ds(r * local, local)
        pairs = (
            (attended_all.at[r], attended_ref.at[r]),
            (features_all.at[r], features_ref.at[r]),
            (branch_all.at[r], branch_ref.at[r]),
            (middle_all.at[r], middle_ref.at[r]),
            (inner_all.at[r], inner_ref.at[lines]),
            (grad_all.at[r], grad_ref.at[lines]),
            (inner_turned.at[r], inner_turned_ref.at[:, lanes]),
            (grad_turned.at[r], grad_turned_ref.at[:, lanes]),
        )
        return [pltpu.make_async_copy(source, target, last_sem.at[r, k]) for k, (source, target) in enumerate(pairs)]

    for r in range(rows):
        for h in range(heads):
            to_self(r, h).wait()
            for m in range(1, 4):
                to_peer(r, h, m).wait()
        for place in range(4):
            for h in range(heads):
                start = (place * heads + h) * size
                flat[start : start + size] = attended_got[r, place, h].astype(F32)
        features = flat[...].astype(BF16)
        features_all[r] = features
        mods = per_token(slot_col[...], seg_all[r, 0], table_ref[r, :, 2 * width :])
        gate_a, shift_b, scale_b, gate_b = (mods[:, k * width : (k + 1) * width] for k in range(4))
        branch = lax.dot_general(features, proj_here[...], (((0,), (0,)), ((), ())), preferred_element_type=F32) + proj_bias[...]
        middle = here[r, 0].astype(F32) + gate_a * branch
        branch_all[r] = branch
        middle_all[r] = middle
        normed = normalize(middle)[0] * (1.0 + scale_b) + shift_b
        grad = cotangent_here[r].astype(F32) * gate_b
        inner_all[r] = normed.astype(BF16)
        grad_all[r] = grad.astype(BF16)
        for values, target in ((normed, inner_turned), (grad, grad_turned)):
            rows_turned[...] = values.T
            for place in range(4):
                for order in range(2):
                    first = pl.multiple_of((2 * place + (core if order == 0 else 1 - core)) * depth, 8)
                    start = (4 * order + place) * depth
                    target[r, start : start + depth] = rows_turned[pl.ds(first, depth), :].astype(BF16)
        sums = jnp.sum(grad.astype(BF16).astype(F32), axis=0, keepdims=True)
        if r == 0:
            bias_sum[...] = sums
        else:
            bias_sum[...] += sums
        go(last_stores(r))
    for r in range(rows):
        for m in range(4):
            end(stores(r, m))
        end(last_stores(r))


def before_feed_forward(slot_col, image_col, seg, fill, conditioning, ada_bias, qv_bias, proj_bias, tokens, ada, weight, proj, cotangent):
    rows, local, width = tokens.shape
    length = 4 * local
    images, slots = conditioning.shape[0], image_col.shape[1]
    heads, size = HEADS // 4, width // HEADS
    columns = ada.shape[0]
    shape = jax.ShapeDtypeStruct
    vmem = lambda dtype, *dims: pltpu.VMEM(dims, dtype)
    near, far = pl.BlockSpec(memory_space=pltpu.VMEM), pl.BlockSpec(memory_space=pl.ANY)
    dma = lambda *dims: pltpu.SemaphoreType.DMA(dims)
    return pl.pallas_call(
        partial(forward_kernel, 512),
        in_specs=[near] * 8 + [far] * 5,
        out_specs=[far] * 10 + [near] * 5,
        out_shape=[
            shape((rows, 4, local, width), BF16),
            shape((rows, 3, heads, size, length), BF16),
            shape((rows, heads, size, length), BF16),
            shape((rows, width, local), BF16),
            shape((rows, local, width), F32),
            shape((rows, local, width), F32),
            shape((rows * local, width), BF16),
            shape((rows * local, width), BF16),
            shape((width, rows * local), BF16),
            shape((width, rows * local), BF16),
            shape((rows, slots, 6 * width), F32),
            shape((rows, 1, length), jnp.int32),
            shape((rows, length, 1), jnp.int32),
            shape((rows, heads, 1, length), F32),
            shape((1, width), F32),
        ],
        scratch_shapes=[
            vmem(BF16, rows, 4, local, width),
            vmem(BF16, rows, 4, local, width),
            vmem(BF16, rows, 3, heads, size, length),
            vmem(BF16, columns, width),
            vmem(BF16, 3, width, 384),
            vmem(F32, 384, width),
            vmem(BF16, 3 * heads * size, width),
            vmem(F32, 384, 8),
            vmem(F32, 4, images, columns),
            vmem(F32, images, 6 * width),
            vmem(jnp.int32, rows, 4, 1, local),
            vmem(BF16, rows, heads, size, length),
            vmem(BF16, rows, 4, heads, size, local),
            vmem(F32, width, local),
            vmem(BF16, rows, width, local),
            vmem(BF16, width, width),
            vmem(BF16, rows, local, width),
            vmem(F32, rows, local, width),
            vmem(F32, rows, local, width),
            vmem(BF16, rows, local, width),
            vmem(BF16, rows, local, width),
            vmem(BF16, rows, width, local),
            vmem(BF16, rows, width, local),
            vmem(F32, width, local),
            dma(6),
            dma(rows),
            dma(3),
            dma(3),
            dma(2 * rows),
            dma(2 * rows),
            dma(2 * rows),
            dma(2 * rows),
            dma(3 * rows * heads),
            dma(3 * rows * heads),
            dma(rows * heads),
            dma(2, 4 * rows),
            dma(rows, 8),
        ],
        compiler_params=pltpu.CompilerParams(vmem_limit_bytes=VMEM_LIMIT, collective_id=6, has_side_effects=True),
        cost_estimate=pl.CostEstimate(flops=2 * 10**10, bytes_accessed=4 * 10**7, transcendentals=0),
    )(slot_col, image_col, seg, fill, conditioning, ada_bias, qv_bias, proj_bias, tokens, ada, weight, proj, cotangent)


def gather_seq(values):
    count = lax.axis_size("seq")
    if count == 4:
        first, second = swap(values, "seq", 1), swap(values, "seq", 2)
        half = values.shape[0] // 2
        third = jnp.concatenate([swap(second[:half], "seq", 1), swap(first[half:], "seq", 2)], axis=0)
        return [values, first, second, third]
    return [values] + [swap(values, "seq", m) for m in range(1, count)]


def exchange_seq(blocks):
    return [blocks[0]] + [swap(blocks[m], "seq", m) for m in range(1, len(blocks))]


def in_order(blocks, axis):
    index = lax.axis_index("seq")
    stacked = jnp.stack(blocks, axis=axis)
    return flip_blocks(stacked, axis, index)


class Halving:
    def __init__(self, blocks, low_first):
        self.blocks = dict(enumerate(blocks))
        bits = [1 << k for k in range(len(blocks).bit_length() - 1)]
        self.bits = bits if low_first else bits[::-1]

    def send(self):
        self.bit = self.bits.pop(0)
        self.kept = [m for m in self.blocks if not m & self.bit]
        return jnp.stack([self.blocks[m | self.bit] for m in self.kept]).astype(BF16)

    def move(self, sent):
        return swap(sent, "seq", self.bit)

    def add(self, came):
        self.blocks = {m: self.blocks[m] + came[k].astype(F32) for k, m in enumerate(self.kept)}


class Spreading:
    def __init__(self, pick):
        chip, chips = lax.axis_index("rows") // 2, lax.axis_size("rows") // 2
        self.own = pick(chip)
        self.sent = [pick(chip ^ m).astype(BF16) for m in range(1, chips)]

    def move(self):
        self.came = [swap(block, "rows", 2 * (m + 1)) for m, block in enumerate(self.sent)]

    def total(self):
        total = self.own
        for block in self.came:
            total = total + block.astype(F32)
        return total


def columns_of(values, index, size):
    return lax.dynamic_slice_in_dim(values, index * size, size, values.ndim - 1)


def lines_of(values, index, size):
    return lax.dynamic_slice_in_dim(values, index * size, size, 0)


def tied(*values):
    return lax.optimization_barrier(values)


def on_square(
    tokens,
    conditioning,
    segment_ids,
    image_index,
    row_fill,
    ada_weight,
    ada_bias,
    qkv_weight,
    qv_bias,
    proj_weight,
    proj_bias,
    up_weight,
    up_bias,
    down_weight,
    down_bias,
    cotangent,
):
    row_count, local_len, width = tokens.shape
    seq_count, groups = lax.axis_size("seq"), lax.axis_size("rows")
    seq_index, row_index = lax.axis_index("seq"), lax.axis_index("rows")
    chips, core = groups // 2, row_index % 2
    full_len = local_len * seq_count
    token_count = row_count * local_len
    heads_dev = HEADS // seq_count
    head_size = width // HEADS
    own = heads_dev * head_size
    image_count = conditioning.shape[0]
    hidden_size = up_weight.shape[1]
    depth = width // groups

    slot_ids = lax.iota(jnp.int32, image_index.shape[1])
    slot_col = jnp.tile(slot_ids, 3)[:, None]
    (
        normed_all,
        packed,
        attended,
        attended_tok,
        branch_a,
        middle,
        normed_b,
        grad_out,
        normed_turned,
        grad_turned,
        slot_mod,
        code_row,
        code_col,
        log_totals,
        part_down_bias,
    ) = before_feed_forward(
        slot_col,
        image_index[:, :, None],
        segment_ids,
        row_fill[:, None],
        conditioning,
        ada_bias[None],
        qv_bias,
        proj_bias.astype(F32)[None],
        tokens,
        ada_weight.T,
        qkv_weight,
        proj_weight,
        cotangent,
    )
    normed_all = normed_all.reshape(row_count, full_len, width)
    cond_wide = conditioning.astype(F32)
    cond_cols = jax.nn.silu(cond_wide).astype(BF16).reshape(image_count, groups, depth).transpose(1, 0, 2)
    seg_row = lax.dynamic_slice_in_dim(segment_ids, seq_index * local_len, local_len, 1)[:, None, :]
    out_sum, grad_sum, part_up_bias, grad_up_weight, down_turned = feed_forward_reduce(
        normed_b, grad_out, normed_turned, grad_turned, up_weight, down_weight, up_bias.astype(F32)
    )
    block_out, grad_middle, slot_sums, part_proj_bias, grad_view, proj_both = after_feed_forward(
        slot_col,
        seg_row,
        slot_mod,
        attended_tok,
        proj_weight,
        down_bias.astype(F32)[None],
        out_sum,
        grad_sum,
        middle,
        branch_a,
        cotangent,
    )
    grad_view = grad_view.reshape(row_count, heads_dev, head_size, full_len)
    grad_sent, qkv_both, grad_proj_weight, grad_down_weight = attend_back_reduce(
        packed, attended, grad_view, log_totals, code_col, code_row, normed_all, proj_both, down_turned, 256, 512
    )
    grad_flat = grad_sent.reshape(row_count, 3 * width, local_len)
    pick = (image_index[:, None, :] == lax.iota(jnp.int32, image_count)[None, :, None]).astype(F32)
    biases = jnp.concatenate(
        [jnp.zeros((2, width), F32), part_proj_bias, part_up_bias.reshape(4, width), part_down_bias], axis=0
    )
    (
        grad_tokens,
        grad_ada_weight,
        grad_cond,
        grad_ada_bias,
        grad_qv_bias,
        grad_proj_bias,
        grad_up_bias,
        grad_down_bias,
        grad_qkv_weight,
    ) = finish_all(
        slot_col,
        seg_row,
        slot_mod,
        grad_flat,
        qkv_weight,
        tokens,
        grad_middle,
        slot_sums,
        pick,
        cond_wide,
        biases,
        qkv_both,
        cond_cols,
        ada_weight.T,
    )
    return (
        block_out,
        grad_tokens,
        grad_cond,
        grad_ada_weight,
        grad_ada_bias[0],
        grad_qkv_weight,
        grad_qv_bias,
        grad_proj_weight,
        grad_proj_bias[0],
        grad_up_weight,
        grad_up_bias[0],
        grad_down_weight.T,
        grad_down_bias[0],
    )


def on_device(
    tokens,
    conditioning,
    segment_ids,
    image_index,
    row_fill,
    ada_weight,
    ada_bias,
    qkv_weight,
    qv_bias,
    proj_weight,
    proj_bias,
    up_weight,
    up_bias,
    down_weight,
    down_bias,
    cotangent,
):
    row_count, local_len, width = tokens.shape
    seq_count, groups = lax.axis_size("seq"), lax.axis_size("rows")
    seq_index, row_index = lax.axis_index("seq"), lax.axis_index("rows")
    chips, core = groups // 2, row_index % 2
    full_len = local_len * seq_count
    token_count = row_count * local_len
    heads_dev = HEADS // seq_count
    head_size = width // HEADS
    own = heads_dev * head_size
    image_count = conditioning.shape[0]
    hidden_size = up_weight.shape[1]
    depth = width // groups

    tokens_all = jnp.concatenate(gather_seq(tokens), axis=1)
    order = lax.iota(jnp.int32, seq_count) ^ seq_index
    seg_blocks = flip_blocks(segment_ids.reshape(row_count, seq_count, local_len), 1, seq_index)
    seg_all = seg_blocks.reshape(row_count, full_len)
    places = (order[:, None] * local_len + lax.iota(jnp.int32, local_len)).reshape(1, full_len)
    codes = jnp.where(places < row_fill[:, None], seg_all, -1 - places)
    code_col, code_row = codes[:, :, None], codes[:, None, :]

    qkv_own = jnp.concatenate(
        [lax.dynamic_slice_in_dim(qkv_weight, part * width + seq_index * own, own, 1).T for part in range(3)], axis=0
    )
    bias_own = lax.dynamic_slice_in_dim(qv_bias.astype(F32), seq_index * own, own, 1)
    bias_own = jnp.concatenate([bias_own[0], jnp.zeros((own,), F32), bias_own[1]])

    cond_wide = conditioning.astype(F32)
    cond_low = jax.nn.silu(cond_wide).astype(BF16)
    mod_part = jnp.dot(cond_low, ada_weight, preferred_element_type=F32)
    modulation = lax.all_gather(mod_part, "seq", axis=1, tiled=True) + ada_bias.astype(F32)
    cond_cols = cond_low.reshape(image_count, groups, depth).transpose(1, 0, 2)
    local_seg = lax.dynamic_slice_in_dim(segment_ids, seq_index * local_len, local_len, 1)
    slot_ids = lax.iota(jnp.int32, image_index.shape[1])
    slot_mod = jnp.take(modulation, image_index, axis=0)

    normed_all, packed = project_qkv(
        tokens_all, seg_all, slot_mod[:, :, : 2 * width], qkv_own, bias_own, heads_dev, min(256, full_len)
    )
    square = seq_count == 4 and chips == 4
    attended, log_totals, *attended_sent = attend(packed, code_col, code_row, 512, square)

    slot_pick = (local_seg[:, :, None] == slot_ids).astype(F32)
    mod_tok = jnp.einsum("rts,rse->rte", slot_pick, slot_mod, precision=lax.Precision.HIGHEST)
    shift_a, scale_a, gate_a, shift_b, scale_b, gate_b = jnp.split(mod_tok, 6, axis=-1)
    tokens_wide = tokens.astype(F32)
    upstream = cotangent.astype(F32)
    grad_branch_b = (upstream * gate_b).astype(BF16)
    part_down_bias = jnp.sum(grad_branch_b.astype(F32), axis=(0, 1))
    grad_out = grad_branch_b.reshape(token_count, width)
    grad_turned = turn_halves(grad_out, seq_count, core)

    def by_block(values):
        return [values[..., m * local_len : (m + 1) * local_len] for m in range(seq_count)]

    if square:
        attended_tok = attended_sent[0]
    else:
        attended_tok = in_order(exchange_seq(by_block(attended.reshape(row_count, own, full_len))), 1)
    attended_tok = attended_tok.reshape(row_count, width, local_len)
    branch_a = jnp.einsum(
        "rft,fe->rte", attended_tok, proj_weight, preferred_element_type=F32
    ) + proj_bias.astype(F32)
    middle = tokens_wide + gate_a * branch_a
    normed_b = modulate(middle, shift_b, scale_b).astype(BF16).reshape(token_count, width)
    normed_turned = turn_halves(normed_b, chips, core)

    if square:
        out_sum, grad_sum, part_up_bias, grad_up_weight, down_turned = feed_forward_reduce(
            normed_b, grad_out, normed_turned, grad_turned, up_weight, down_weight, up_bias.astype(F32)
        )
        part_up_bias = part_up_bias.reshape(1, hidden_size)
    else:
        out_sum, grad_sum, up_keep, up_send, down_keep, down_send, part_up_bias = feed_forward(
            normed_b, grad_out, normed_turned, grad_turned, up_weight, down_weight, up_bias.astype(F32)[None], 512
        )
        up_came, down_came = swap(up_send, "rows", 1), swap(down_send, "rows", 1)
    branch_b = out_sum.reshape(row_count, local_len, width) + down_bias.astype(F32)
    grad_normed_b = grad_sum.reshape(row_count, local_len, width)
    block_out = (middle + gate_b * branch_b).astype(BF16)
    grad_gate_b = upstream * branch_b
    _, norm_back_b = jax.vjp(modulate, middle, shift_b, scale_b)
    grad_mid_norm, grad_shift_b, grad_scale_b = norm_back_b(grad_normed_b)
    grad_middle = upstream + grad_mid_norm
    grad_branch_a = (grad_middle * gate_a).astype(BF16)
    grad_gate_a = grad_middle * branch_a
    part_proj_bias = jnp.sum(grad_branch_a.astype(F32), axis=(0, 1))
    grad_attended = jnp.einsum(
        "fe,rte->rft", proj_weight, grad_branch_a, preferred_element_type=F32
    ).astype(BF16)
    heads_blocks = [lax.dynamic_slice_in_dim(grad_attended, (seq_index ^ m) * own, own, 1) for m in range(seq_count)]
    grad_heads_in = jnp.concatenate(exchange_seq(heads_blocks), axis=2)
    grad_view = grad_heads_in.reshape(row_count, heads_dev, head_size, full_len)

    part_proj = jnp.einsum("rte,rft->ef", grad_branch_a, attended_tok, preferred_element_type=F32)
    proj_view = part_proj.reshape(seq_count, 2, depth * groups // (2 * seq_count), width)
    proj_keep = lax.dynamic_index_in_dim(proj_view, core, 1, keepdims=False)
    proj_send = lax.dynamic_index_in_dim(proj_view, 1 - core, 1, keepdims=False).astype(BF16)
    proj_came = swap(proj_send, "rows", 1).reshape(width // 2, width)
    proj_keep = proj_keep.reshape(width // 2, width)
    up_size, down_size = hidden_size // seq_count, width // (2 * seq_count)
    proj_blocks = [
        lines_of(proj_keep, seq_index ^ m, down_size) + lines_of(proj_came, seq_index ^ m, down_size).astype(F32)
        for m in range(seq_count)
    ]
    if square:
        proj_sent = [block.astype(BF16) for block in proj_blocks[1:]]
        grad_view, *proj_sent = tied(grad_view, *proj_sent)
        proj_total = proj_blocks[0]
        for m in range(1, seq_count):
            proj_total = proj_total + swap(proj_sent[m - 1], "seq", m).astype(F32)
    else:
        ups = Halving(
            [
                columns_of(up_keep, seq_index ^ m, up_size) + columns_of(up_came, seq_index ^ m, up_size).astype(F32)
                for m in range(seq_count)
            ],
            True,
        )
        downs = Halving(
            [
                jnp.concatenate(
                    [
                        lines_of(down_keep, seq_index ^ m, down_size)
                        + lines_of(down_came, seq_index ^ m, down_size).astype(F32),
                        proj_blocks[m],
                    ],
                    axis=1,
                )
                for m in range(seq_count)
            ],
            False,
        )
        up_sent, down_sent = ups.send(), downs.send()
        up_came, down_came = ups.move(up_sent), downs.move(down_sent)

    grad_heads, *grad_sent = attend_back(
        packed, attended, grad_view, log_totals, code_col, code_row, 256, 512, square
    )
    grad_own = grad_heads.reshape(row_count, 3 * own, full_len)
    if square:
        grad_flat = grad_sent[0]
    else:
        grad_blocks = exchange_seq(by_block(grad_own))
        grad_flat = in_order([block.reshape(row_count, 3, own, local_len) for block in grad_blocks], 2)
    grad_flat = grad_flat.reshape(row_count, 3 * width, local_len)

    qkv_keep, qkv_send, own_sums = qkv_weight_grad(grad_own, normed_all)
    down_part, proj_part = hidden_size // chips, width // chips
    if square:
        proj_spread = Spreading(lambda chip: columns_of(proj_total, chip, proj_part))
        grad_flat, qkv_send, *proj_spread.sent = tied(grad_flat, qkv_send, *proj_spread.sent)
        proj_spread.move()
    else:
        while ups.bits:
            ups.add(up_came)
            downs.add(down_came)
            up_came, down_came = ups.move(ups.send()), downs.move(downs.send())
        ups.add(up_came)
        downs.add(down_came)
        up_total, down_total = ups.blocks[0], downs.blocks[0][:, :hidden_size]
        proj_total = downs.blocks[0][:, hidden_size:]
        up_spread = Spreading(lambda chip: lines_of(up_total, chip, depth))
        down_spread = Spreading(
            lambda chip: jnp.concatenate(
                [columns_of(down_total, chip, down_part), columns_of(proj_total, chip, proj_part)], axis=1
            )
        )
        up_spread.move()
        down_spread.move()
    qkv_came = swap(qkv_send, "rows", 1)
    grad_normed_a = jnp.einsum("rft,df->rtd", grad_flat, qkv_weight, preferred_element_type=F32)
    _, norm_back_a = jax.vjp(modulate, tokens_wide, shift_a, scale_a)
    grad_tok_norm, grad_shift_a, grad_scale_a = norm_back_a(grad_normed_a)
    grad_tokens = grad_middle + grad_tok_norm
    grad_mod_tok = jnp.concatenate(
        [grad_shift_a, grad_scale_a, grad_gate_a, grad_shift_b, grad_scale_b, grad_gate_b], axis=-1
    )
    slot_grads = jnp.einsum("rts,rte->rse", slot_pick, grad_mod_tok, precision=lax.Precision.HIGHEST)
    image_pick = (image_index[:, :, None] == lax.iota(jnp.int32, image_count)).astype(F32)
    grad_modulation = jnp.einsum("rsi,rse->ie", image_pick, slot_grads, precision=lax.Precision.HIGHEST)

    own_sums = own_sums.reshape(3, own)
    part_qv = lax.dynamic_update_slice(
        jnp.zeros((2, width), F32), jnp.stack([own_sums[0], own_sums[2]]), (0, seq_index * own)
    )
    small = jnp.concatenate([part_qv.reshape(-1), part_proj_bias, part_up_bias[0], part_down_bias])
    columns = ada_weight.shape[1]
    lines = -(-small.size // (seq_count * columns))
    room = seq_count * columns * lines
    small = jnp.pad(small, (0, room - small.size)).reshape(seq_count, lines, columns)
    mod_view = grad_modulation.reshape(image_count, seq_count, columns).transpose(1, 0, 2)
    joined = jnp.concatenate(
        [mod_view, jnp.zeros((seq_count, 1, columns), F32), small, jnp.zeros((seq_count, 7 - lines, columns), F32)], axis=1
    )
    qkv_both = qkv_keep + qkv_came.astype(F32)
    qkv_spread = Spreading(lambda chip: lax.dynamic_index_in_dim(qkv_both, chip, 0, keepdims=False))
    joined, *qkv_spread.sent = tied(joined, *qkv_spread.sent)
    qkv_spread.move()
    if square:
        turned = jnp.concatenate([down_turned, proj_spread.total()], axis=1)
    else:
        grad_up_weight, turned = up_spread.total(), down_spread.total()
    half = down_part // 2
    cut = lambda index: jnp.concatenate(
        [columns_of(turned[:, :down_part], index, half), columns_of(turned[:, down_part:], index, proj_part // 2)], axis=1
    )
    core_keep, core_sent = cut(core), cut(1 - core)
    joined, core_sent = tied(joined, core_sent)
    core_came = swap(core_sent, "rows", 1)
    grad_ada_weight, cond_sum, bias_sums = finish(joined, ada_weight, cond_cols, image_count)
    _, silu_back = jax.vjp(jax.nn.silu, cond_wide)
    grad_cond = silu_back(cond_sum)[0]
    grad_ada_bias = bias_sums[:, 0].reshape(-1)
    small = bias_sums[:, 1 : 1 + lines].reshape(-1)
    grad_qv_bias = small[: 2 * width].reshape(2, width)
    grad_proj_bias = small[2 * width : 3 * width]
    grad_up_bias = small[3 * width : 3 * width + hidden_size]
    grad_down_bias = small[3 * width + hidden_size : 4 * width + hidden_size]

    pair = flip_blocks(jnp.stack([core_keep, core_came]), 0, core).reshape(-1, core_keep.shape[1])
    grad_down_weight, grad_proj_weight = pair[:, :half].T, pair[:, half:].T

    qkv_total = qkv_spread.total()
    pieces = []
    for place in range(3):
        pairs = [((3 * target + place) % seq_count, target) for target in range(seq_count)]
        part_of = [0] * seq_count
        for source, target in pairs:
            part_of[source] = (3 * target + place) // seq_count
        chosen = columns_of(qkv_total, jnp.array(part_of, jnp.int32)[seq_index], own)
        pieces.append(lax.ppermute(chosen, "seq", pairs))
    grad_qkv_weight = jnp.concatenate(pieces, axis=1)
    return (
        block_out,
        grad_tokens,
        grad_cond,
        grad_ada_weight,
        grad_ada_bias,
        grad_qkv_weight,
        grad_qv_bias,
        grad_proj_weight,
        grad_proj_bias,
        grad_up_weight,
        grad_up_bias,
        grad_down_weight,
        grad_down_bias,
    )


def solution(mesh):
    in_specs = (
        P("rows", "seq", None),
        P("rows", None),
        P("rows", None),
        P("rows", None),
        P("rows"),
        P(None, "seq"),
        P(),
        P(),
        P(),
        P(),
        P(),
        P(),
        P(),
        P(),
        P(),
        P("rows", "seq", None),
    )
    out_specs = (
        P("rows", "seq", None),
        P("rows", "seq", None),
        P("rows", None),
        P("rows", "seq"),
        P(),
        P("rows", "seq"),
        P(),
        P("rows", "seq"),
        P(),
        P("rows", "seq"),
        P(),
        P("rows", "seq"),
        P(),
    )
    square = mesh.shape["seq"] == 4 and mesh.shape["rows"] == 8
    return jax.shard_map(
        on_square if square else on_device, mesh=mesh, in_specs=in_specs, out_specs=out_specs, check_vma=False
    )
```

profile of v0, /device:TPU:0, one launch (start us, length us, event | category | flops | bytes accessed | tf_op | source)
XLA Modules:
  0.0 344.5 jit_solution(6144452386817537265)
XLA Ops:
  0.7 0.7 broadcast_in_dim_tile.8.slot_col
  1.3 1.3 broadcast_in_dim.30.ada_bias
  2.7 1.4 copy.35.image_col
  4.0 1.3 reshape.54.proj_bias
  5.3 1.3 copy.36.fill
  6.6 0.0 copy-start.10
  6.6 75.3 %shard_map.255 = (bf16[2,4,256,1152]{3,2,1,0:T(8,128)(2,1)}, bf16[2,3,4,72,1024]{4,3,2,1,0:T(8,128)(2,1)}, bf16[2,4,72,1024]{3,2,1,0:T(8,128)(2,1)}, bf16[2,1152...) custom-call(s32[24,1]{1,0:T(8,128)} %broadcast_in_dim_tile.8.slot_co, ...), custom_call_target="tpu_custom_call" | custom-call | flops 20000000000 | bytes 40000000 | tf_op jit(solution)/shard_map/pallas_call | solution.py:1928
  81.9 0.0 copy-done.10
  81.9 0.6 reshape.57.bias
  82.5 0.0 copy-start.14
  82.5 112.9 %shard_map.256 = (f32[512,1152]{1,0:T(8,128)}, f32[512,1152]{1,0:T(8,128)}, f32[4,1,1152]{2,1,0:T(1,128)}, f32[144,1152]{1,0:T(8,128)}, f32[144,1152]{1,0:T(8,128)}) custom-call(bf16[512,1152]{1,0:T(8,128)(2,1)} %get-tuple-element.54.normed, bf16[512,1152]{1,0:T(8,128)(2,1)} %get-tuple-element.55.grad_out, ...), custom_call_target="tpu_custom_call" | custom-call | flops 32614907904 | bytes 31850496 | tf_op jit(solution)/shard_map/pallas_call | solution.py:658
  195.4 0.7 constant_dynamic-slice_fusion
  196.1 0.6 broadcast_in_dim.27.seg
  196.7 0.0 copy-done.14
  196.7 0.6 reshape.55.bias
  197.3 0.0 copy-start.9
  197.3 0.0 copy-start.12
  197.3 25.2 %shard_map.257 = (bf16[2,256,1152]{2,1,0:T(8,128)(2,1)}, f32[2,256,1152]{2,1,0:T(8,128)}, f32[2,8,4608]{2,1,0:T(8,128)}, f32[1,1152]{1,0:T(1,128)}, bf16[2,288,1...) custom-call(s32[24,1]{1,0:T(8,128)} %broadcast_in_dim_tile.8.slot_col, s32[2,1,256]{2,1,0:T(1,128)} %broadcast_in_dim.27.seg, ...), custom_call_target="tpu_custom_call" | custom-call | flops 8000000000 | bytes 30000000 | tf_op jit(solution)/shard_map/pallas_call | solution.py:864
  222.5 0.0 copy-done.9
  222.5 0.0 copy-done.12
  222.5 1.4 pad_maximum_fusion.biases
  223.9 0.0 copy-start.7
  223.9 0.0 copy-start.13
  223.9 56.0 %shard_map.258 = (bf16[2,3,4,4,72,256]{5,4,3,2,1,0:T(8,128)(2,1)}, f32[4,144,864]{2,1,0:T(8,128)}, f32[144,288]{1,0:T(8,128)}, f32[288,576]{1,0:T(8,128)}) custom-call(s32[2,1024,1]{2,1,0:T(8,128)} %get-tuple-element.63.code_col, s32[2,1,1024]{2,1,0:T(1,128)} %get-tuple-element.64.code_row, bf16[2,3,4,72,1024]{4,3,2,1,0:T(8,128)(2,1)} %get-tuple-element.65.query.key.value, ...), custom_call_target="tpu_custom_call" | custom-call | flops 21474836480 | bytes 9437184 | tf_op jit(solution)/shard_map/pallas_call | solution.py:1288
  280.0 0.0 copy-done.7
  280.0 0.1 reshape.53
  280.1 0.6 copy.43
  280.8 0.6 convert_element_type.13.conditioning
  281.4 0.0 copy-done.13
  281.4 0.6 fusion.pick
  282.0 0.0 copy-start.1
  282.0 48.9 %shard_map.259 = (f32[2,256,1152]{2,1,0:T(8,128)}, f32[144,1728]{1,0:T(8,128)}, f32[16,1152]{1,0:T(8,128)}, f32[1,6912]{1,0:T(1,128)}, f32[2,1152]{1,0:T(2,128)}...) custom-call(s32[24,1]{1,0:T(8,128)} %broadcast_in_dim_tile.8.slot_col, ...), custom_call_target="tpu_custom_call" | custom-call | flops 5000000000 | bytes 30000000 | tf_op jit(solution)/shard_map/pallas_call | solution.py:1574
  330.9 0.0 copy-start
  330.9 1.6 reduce
  332.5 1.4 reduce.2
  333.9 1.3 reduce.1
  335.2 1.3 reduce.3
  336.5 0.0 copy-done.1
  336.5 1.0 copy.54
  337.5 0.0 copy-done
  337.5 0.0 copy-start.8
  337.5 0.0 copy-start.2
  337.5 0.0 copy-start.5
  337.5 1.4 copy.55
  338.9 0.0 copy-done.8
  338.9 0.0 copy-start.11
  338.9 0.0 copy-start.6
  338.9 0.0 copy-start.4
  338.9 0.6 copy.56
  339.6 0.0 copy-done.2
  339.6 0.0 copy-start.3
  339.6 1.0 copy.57
  340.5 0.0 copy-done.5
  340.5 0.8 copy.58
  341.3 0.0 copy-done.11
  341.3 0.6 copy.59
  341.9 0.0 copy-done.6
  341.9 0.7 copy.60
  342.6 0.0 copy-done.4
  342.6 0.8 copy.61
  343.5 0.0 copy-done.3
  343.5 0.9 copy.62
  (5 shorter events, 0.0 us)
Async XLA Ops:
  6.6 75.3 %copy-start.10 = (bf16[4608]{0:T(1024)(128)(2,1)S(1)}, bf16[4608]{0:T(1024)(128)(2,1)}, u32[]{:S(2)}) copy-start(bf16[4608]{0:T(1024)(128)(2,1)} %param.28) | copy-start | bytes 27652
  82.5 114.2 %copy-start.14 = (bf16[1152]{0:T(1024)(128)(2,1)S(1)}, bf16[1152]{0:T(1024)(128)(2,1)}, u32[]{:S(2)}) copy-start(bf16[1152]{0:T(1024)(128)(2,1)} %param.30) | copy-start | bytes 6916
  197.3 25.2 %copy-start.9 = (f32[4,1,1152]{2,1,0:T(1,128)S(1)}, f32[4,1,1152]{2,1,0:T(1,128)}, u32[]{:S(2)}) copy-start(f32[4,1,1152]{2,1,0:T(1,128)} %get-tuple-element.76) | copy-start | bytes 55300
  197.3 25.2 %copy-start.12 = (f32[1,1152]{1,0:T(1,128)S(1)}, f32[1,1152]{1,0:T(1,128)}, u32[]{:S(2)}) copy-start(f32[1,1152]{1,0:T(1,128)} %get-tuple-element.77) | copy-start | bytes 13828
  223.9 56.1 %copy-start.7 = (bf16[16,1152]{1,0:T(8,128)(2,1)S(1)}, bf16[16,1152]{1,0:T(8,128)(2,1)}, u32[]{:S(2)}) copy-start(bf16[16,1152]{1,0:T(8,128)(2,1)} %conditioning.1) | copy-start | bytes 110596
  223.9 57.5 %copy-start.13 = (s32[2,8]{1,0:T(2,128)S(1)}, s32[2,8]{1,0:T(2,128)}, u32[]{:S(2)}) copy-start(s32[2,8]{1,0:T(2,128)} %param.19) | copy-start | bytes 196
  282.0 54.5 %copy-start.1 = (bf16[2,256,1152]{2,1,0:T(8,128)(2,1)S(1)}, bf16[2,256,1152]{2,1,0:T(8,128)(2,1)}, u32[]{:S(2)}) copy-start(bf16[2,256,1152]{2,1,0:T(8,128)(2,1)} %get-tuple-element.104) | copy-start | bytes 3538948
  330.9 6.6 %copy-start = (f32[2,256,1152]{2,1,0:T(8,128)S(1)}, f32[2,256,1152]{2,1,0:T(8,128)}, u32[]{:S(2)}) copy-start(f32[2,256,1152]{2,1,0:T(8,128)} %get-tuple-element.105) | copy-start | bytes 7077892
  337.5 1.4 copy-start.8
  337.5 2.1 copy-start.2
  337.5 3.0 copy-start.5
  338.9 2.4 copy-start.11
  338.9 3.0 copy-start.6
  338.9 3.7 %copy-start.4 = (f32[144,1152]{1,0:T(8,128)S(1)}, f32[144,1152]{1,0:T(8,128)}, u32[]{:S(2)}) copy-start(f32[144,1152]{1,0:T(8,128)} %get-tuple-element.113) | copy-start | bytes 1990660
  339.6 3.9 %copy-start.3 = (f32[288,576]{1,0:T(8,128)S(1)}, f32[288,576]{1,0:T(8,128)}, u32[]{:S(2)}) copy-start(f32[288,576]{1,0:T(8,128)} %get-tuple-element.89) | copy-start | bytes 1990660
where the time goes:
time: 351 us; the launch traced here: 345 us
  Pallas kernels  318 us (91%)
  local copies, waits for them, and re-layouts  17.1 us (5%)
  other arithmetic  8.21 us (2%)
    pallas_call x1, Pallas kernels, feed_forward_reduce(): pl.pallas_call(partial(mlp_reduce_kernel, tiles), grid=(tiles + STAGES,),...  113 us
    pallas_call x1, Pallas kernels, before_feed_forward(): pl.pallas_call(partial(forward_kernel, 512), in_specs=[near] * 8 + [far]...  75.3 us
    pallas_call x1, Pallas kernels, attend_back_reduce(): pl.pallas_call(partial(attend_back_reduce_kernel, block, inner, size ** (...  56 us
    pallas_call x1, Pallas kernels, finish_all(): pl.pallas_call(last_kernel, grid=(rows,), in_specs=[fixed(*slot_col.shape...  48.9 us
    pallas_call x1, Pallas kernels, after_feed_forward(): pl.pallas_call(after_kernel, grid=(rows,), in_specs=[fixed(*slot_col.shap...  25.2 us
    unnamed x40, local copies, waits for them, and re-layouts  7.85 us

commit v1 on v0

--- a/solution.py
+++ b/solution.py
@@ -473,6 +473,7 @@
     last_came,
     chip_sent,
     chip_came,
+    bias_line,
 ):
     step = pl.program_id(0)
     seq, row = lax.axis_index("seq"), lax.axis_index("rows")
@@ -487,6 +488,7 @@
 
     @pl.when(step == 0)
     def _():
+        bias_line[...] = bias[...].astype(F32).reshape(1, bias.shape[0])
         barrier = pltpu.get_barrier_semaphore()
         for peer in (core_peer, x_peer, y_peer, *chip_peers[1:]):
             pl.semaphore_signal(barrier, inc=1, device_id=peer, device_id_type=pl.DeviceIdType.MESH)
@@ -594,7 +596,14 @@
         slot = lax.rem(step, 2)
         up = jnp.concatenate([up0[...], up1[...], up2[...], up3[...]], axis=1)
         down = jnp.concatenate([down0[...], down1[...], down2[...], down3[...]], axis=0)
-        biases = jnp.concatenate([bias[owner] for owner in range(4)], axis=1)
+        hidden_part = bias.shape[0] // 4
+        biases = jnp.concatenate(
+            [
+                bias_line[:, pl.ds(pl.multiple_of(owner * hidden_part + step * 128, 128), 128)]
+                for owner in range(4)
+            ],
+            axis=1,
+        )
         c0 = math.sqrt(2 / math.pi)
         c1 = c0 * 0.044715
         hidden = jnp.dot(normed[...], up, preferred_element_type=F32) + biases
@@ -661,7 +670,7 @@
         in_specs=[fixed(count, width), fixed(count, width), fixed(width, count), fixed(width, count)]
         + [up_block(owner) for owner in range(4)]
         + [down_block(owner) for owner in range(4)]
-        + [bias_block],
+        + [pl.BlockSpec((hidden,), lambda t: (0,))],
         out_specs=[
             result(count, width),
             result(count, width),
@@ -700,14 +709,19 @@
             pair(BF16, 3, 2, quarter, 128),
         ]
         + [pltpu.SemaphoreType.DMA((2, 2))] * 6
-        + [pltpu.SemaphoreType.DMA((3, 2))] * 2,
+        + [pltpu.SemaphoreType.DMA((3, 2))] * 2
+        + [pltpu.VMEM((1, hidden), F32)],
         compiler_params=pltpu.CompilerParams(collective_id=1, has_side_effects=True, vmem_limit_bytes=VMEM_LIMIT),
         cost_estimate=pl.CostEstimate(
             flops=12 * count * width * hidden,
             bytes_accessed=6 * width * hidden,
             transcendentals=count * hidden,
         ),
-    )(normed, grad_out, normed_turned, grad_turned, up, up, up, up, down, down, down, down, bias.reshape(4, 1, part))
+    )(normed, grad_out, normed_turned, grad_turned, up, up, up, up, down, down, down, down, bias)
+
+
+def slot_column(slots):
+    return lax.rem(lax.broadcasted_iota(jnp.int32, (3 * slots, 1), 0), slots)
 
 
 def split_low(values):
@@ -741,7 +755,6 @@
 
 
 def after_kernel(
-    slot_col,
     seg,
     table,
     attended,
@@ -757,7 +770,8 @@
     slot_sums,
     bias_sum,
     view_ref,
-    proj_ref,
+    proj_own,
+    proj_low,
     heads_out,
     total,
     core_out,
@@ -791,7 +805,9 @@
     def to_self(r):
         return pltpu.make_async_copy(heads_out.at[r, seq], view_ref.at[r, :, pl.ds(0, length)], kept.at[r])
 
-    mods = per_token(slot_col[...], seg[0], table[0, :, 2 * width :])
+    slot_col = slot_column(table.shape[1])
+    seg_row = seg[pl.ds(step, 1), pl.ds(pl.multiple_of(seq * length, 128), length)]
+    mods = per_token(slot_col, seg_row, table[0, :, 2 * width :])
     gate_a, scale_b, gate_b = (mods[:, k * width : (k + 1) * width] for k in (0, 2, 3))
     middle, branch = middle_ref[0], branch_ref[0]
     upstream = cotangent[0].astype(F32)
@@ -836,25 +852,28 @@
             core_out[chip] = total[pl.ds(other, depth), :].astype(BF16)
         to_core.start()
 
-    branch_b = out_sum[...] + bias[...]
+    branch_b = out_sum[...] + bias[...].astype(F32).reshape(1, width)
     block_out[0] = (middle + gate_b * branch_b).astype(BF16)
     pieces = (grad_middle * branch, grad_normed, grad_normed * normal, upstream * branch_b)
     for k, piece in enumerate(pieces):
-        slot_sums[0, :, k * width : (k + 1) * width] = per_slot(slot_col[...], seg[0], piece)
+        slot_sums[0, :, k * width : (k + 1) * width] = per_slot(slot_col, seg_row, piece)
 
     @pl.when(step == rows - 1)
     def _():
         to_core.wait()
         for chip in range(4):
             mine = pl.multiple_of((2 * chip + core) * depth, 8)
-            proj_ref[chip] = total[pl.ds(mine, depth), :] + core_got[chip].astype(F32)
+            proj_low[chip] = (total[pl.ds(mine, depth), :] + core_got[chip].astype(F32)).astype(BF16)
+        chip = lax.div(row, 2)
+        mine = pl.multiple_of(row * depth, 8)
+        proj_own[...] = total[pl.ds(mine, depth), :] + core_got[chip].astype(F32)
         for r in range(heads_out.shape[0]):
             to_self(r).wait()
             for m in range(1, 4):
                 to_peer(r, m).wait()
 
 
-def after_feed_forward(slot_col, seg, table, attended, weight, bias, out_sum, grad_sum, middle, branch, cotangent):
+def after_feed_forward(seg, table, attended, weight, bias, out_sum, grad_sum, middle, branch, cotangent):
     rows, length, width = cotangent.shape
     slots = table.shape[1]
     depth = width // 8
@@ -865,12 +884,11 @@
         after_kernel,
         grid=(rows,),
         in_specs=[
-            fixed(*slot_col.shape),
-            row(1, length),
+            fixed(*seg.shape),
             row(*table.shape[1:]),
             row(width, length),
             fixed(width, width),
-            fixed(1, width),
+            fixed(width),
             pl.BlockSpec((length, width), lambda r: (r, 0)),
             pl.BlockSpec((length, width), lambda r: (r, 0)),
             row(length, width),
@@ -883,6 +901,7 @@
             row(slots, 4 * width),
             fixed(1, width),
             pl.BlockSpec(memory_space=pl.ANY),
+            fixed(depth, width),
             fixed(4, depth, width),
         ],
         out_shape=[
@@ -891,7 +910,8 @@
             shape((rows, slots, 4 * width), F32),
             shape((1, width), F32),
             shape((rows, width // 4, 4 * length), BF16),
-            shape((4, depth, width), F32),
+            shape((depth, width), F32),
+            shape((4, depth, width), BF16),
         ],
         scratch_shapes=[
             pltpu.VMEM((rows, 4, width // 4, length), BF16),
@@ -906,7 +926,7 @@
         ],
         compiler_params=pltpu.CompilerParams(vmem_limit_bytes=VMEM_LIMIT, collective_id=4, has_side_effects=True),
         cost_estimate=pl.CostEstimate(flops=8 * 10**9, bytes_accessed=3 * 10**7, transcendentals=0),
-    )(slot_col, seg, table, attended, weight, bias, out_sum, grad_sum, middle, branch, cotangent)
+    )(seg, table, attended, weight, bias, out_sum, grad_sum, middle, branch, cotangent)
 
 
 def qkv_weight_kernel(grad, normed, keep_ref, send_ref, sum_ref, total, turned):
@@ -1093,7 +1113,7 @@
     )
 
 
-def attend_back_reduce_kernel(
+def back_kernel(
     block,
     inner,
     scale,
@@ -1106,82 +1126,164 @@
     grad_out,
     lse,
     normed,
-    proj,
+    proj_own,
+    proj_low,
     down,
-    token_ref,
-    qkv_ref,
+    seg,
+    table,
+    slot_sums,
+    image_index,
+    conditioning,
+    proj_bias,
+    up_bias,
+    down_bias,
+    tokens,
+    grad_middle,
+    weight,
+    ada,
+    grad_tokens,
     proj_ref,
     down_ref,
+    ada_ref,
+    cond_ref,
+    ada_bias_ref,
+    qv_bias_ref,
+    proj_bias_ref,
+    up_bias_ref,
+    down_bias_ref,
+    qkv_ref,
     grads,
+    token_got,
     key_sum,
     value_sum,
     keys,
     values,
-    flat,
     total,
-    turned,
+    spare,
     core_out,
     core_got,
-    proj_out,
     proj_got,
     seq_out,
     seq_got,
     down_out,
     down_got,
+    qkv_own,
+    chip_got,
+    weights,
+    tokens_here,
+    middle_here,
+    grad_here,
+    features,
+    image_sums,
+    feature_sums,
+    mod,
+    got,
+    lines,
+    lines_got,
+    low_all,
+    small_core,
+    small_chip,
+    small_seq,
+    cond_all,
+    cond,
+    column_got,
+    piece_out,
+    piece_got,
     sent,
     came,
     kept,
-    proj_sent,
-    proj_came,
-    seq_sent,
-    seq_came,
-    core_sent,
-    core_came,
+    load_sem,
+    store_sem,
+    other_sent,
+    other_came,
 ):
     length, size = query.shape[-1], query.shape[-2]
     row, head = pl.program_id(0), pl.program_id(1)
     rows, _, heads = grads.shape[:3]
     width = normed.shape[-1]
+    images, columns = mod.shape[1:]
     depth, own, local = width // 8, width // 4, length // 4
     seq, group = lax.axis_index("seq"), lax.axis_index("rows")
     chip, core = lax.div(group, 2), lax.rem(group, 2)
-    peers = [{"seq": peer} for peer in peers_of(seq)]
+    seq_places = peers_of(seq)
+    peers = [{"seq": place} for place in seq_places]
+    row_places = [lax.rem(group + m, 8) for m in range(8)]
+    row_peers = [{"rows": place} for place in row_places]
     core_peer = {"rows": group + 1 - 2 * core}
     to_chip = [lax.rem(chip + k, 4) for k in range(4)]
+    from_chip = [lax.rem(chip + 4 - k, 4) for k in range(4)]
     chip_peers = [{"rows": 2 * to_chip[k] + core} for k in range(4)]
     first = (row == 0) & (head == 0)
     last = (row == rows - 1) & (head == heads - 1)
+    slot_col = slot_column(table.shape[1])
+    used = [0]
+
+    def copy_to(source, target, device):
+        used[0] += 1
+        return send_to(source, target, other_sent.at[used[0] - 1], other_came.at[used[0] - 1], device)
+
+    def go(copies):
+        for copy in copies:
+            copy.start()
+
+    def end(copies):
+        for copy in copies:
+            copy.wait()
 
     def to_peer(r, h, m):
         place = (r * heads + h) * 3 + m - 1
         source = grads.at[r, :, h, :, pl.ds(m * local, local)]
-        return send_to(source, token_ref.at[r, :, seq, h], sent.at[place], came.at[place], peers[m - 1])
+        return send_to(source, token_got.at[r, :, seq, h], sent.at[place], came.at[place], peers[m - 1])
 
     def to_self(r, h):
         source = grads.at[r, :, h, :, pl.ds(0, local)]
-        return pltpu.make_async_copy(source, token_ref.at[r, :, seq, h], kept.at[r * heads + h])
-
-    proj_copies = [
-        send_to(proj_out.at[to_chip[k]], proj_got.at[k - 1], proj_sent.at[k - 1], proj_came.at[k - 1], chip_peers[k])
-        for k in range(1, 4)
+        return pltpu.make_async_copy(source, token_got.at[r, :, seq, h], kept.at[r * heads + h])
+
+    proj_copies = [copy_to(proj_low.at[to_chip[k]], proj_got.at[k - 1], chip_peers[k]) for k in range(1, 4)]
+    seq_copies = [copy_to(seq_out.at[place], seq_got.at[m], peers[m]) for m, place in enumerate(seq_places)]
+    core_copy = copy_to(core_out, core_got, core_peer)
+    down_copy = copy_to(down_out.at[1 - core], down_got, core_peer)
+    chip_copies = [copy_to(core_out.at[to_chip[k]], chip_got.at[k - 1], chip_peers[k]) for k in range(1, 4)]
+    column_copies = [copy_to(cond.at[row_places[m]], column_got.at[group], row_peers[m]) for m in range(1, 8)]
+    mod_copies = [copy_to(mod.at[place], got.at[m], peers[m]) for m, place in enumerate(seq_places)]
+    line_copies = [copy_to(lines.at[place], lines_got.at[m], peers[m]) for m, place in enumerate(seq_places)]
+    low_core = copy_to(low_all.at[chip, core], low_all.at[chip, core], core_peer)
+    low_chips = [copy_to(low_all.at[chip, core], low_all.at[chip, core], chip_peers[k]) for k in range(1, 4)]
+    low_on = [copy_to(low_all.at[from_chip[k], core], low_all.at[from_chip[k], core], core_peer) for k in range(1, 4)]
+    small_over = copy_to(small_core.at[core], small_core.at[core], core_peer)
+    small_chips = [copy_to(small_chip.at[chip], small_chip.at[chip], chip_peers[k]) for k in range(1, 4)]
+    small_copies = [copy_to(small_seq.at[seq], small_seq.at[seq], peers[m]) for m in range(3)]
+    cond_copies = [copy_to(cond_all.at[seq], cond_all.at[seq], peers[m]) for m in range(3)]
+    base = used[0]
+
+    load_weights = [
+        pltpu.make_async_copy(weight.at[:, pl.ds(part * width, width)], weights.at[part], load_sem.at[part])
+        for part in range(3)
     ]
-    seq_copies = [
-        send_to(seq_out.at[target], seq_got.at[m], seq_sent.at[m], seq_came.at[m], peers[m])
-        for m, target in enumerate(peers_of(seq))
+    load_tokens = pltpu.make_async_copy(tokens, tokens_here, load_sem.at[3])
+    load_middle = pltpu.make_async_copy(grad_middle, middle_here, load_sem.at[4])
+    load_ada = [
+        pltpu.make_async_copy(ada.at[pl.ds(0, width)], weights.at[0], load_sem.at[5]),
+        pltpu.make_async_copy(ada.at[pl.ds(width, columns - width)], weights.at[1, pl.ds(0, columns - width)], load_sem.at[6]),
     ]
-    core_copy = send_to(core_out, core_got, core_sent.at[0], core_came.at[0], core_peer)
-    down_copy = send_to(down_out.at[1 - core], down_got, core_sent.at[1], core_came.at[1], core_peer)
 
     @pl.when(first)
     def _():
-        greet(peers + [core_peer] + chip_peers[1:])
-        proj_out[...] = proj[...].astype(BF16)
-        for copy in proj_copies:
-            copy.start()
+        greet(peers + row_peers[1:])
+        go(proj_copies)
         half = down.shape[1] // 2
         for place in range(2):
             down_out[place] = down[:, place * half : (place + 1) * half]
         down_copy.start()
+        go(load_weights + [load_tokens, load_middle])
+        value = conditioning[...].astype(F32)
+        low = (value / (1.0 + jnp.exp(-value))).astype(BF16)
+        for place in range(8):
+            cond[place] = low[:, place * depth : (place + 1) * depth]
+        column_got[group] = cond[group]
+        go(column_copies)
+        image_sums[...] = jnp.zeros_like(image_sums)
+        feature_sums[...] = jnp.zeros_like(feature_sums)
 
     keys[...] = key[0, 0].astype(F32).T.astype(BF16)
     values[...] = value[0, 0].astype(F32).T.astype(BF16)
@@ -1215,40 +1317,77 @@
             grad_query += jnp.dot(key[0, 0, :, there], grad_raw, preferred_element_type=F32)
         low = grad_query.astype(BF16)
         grads[row, 0, head, :, here] = low
-        flat[place_of(0), here] = low.astype(F32)
+        spare[place_of(0), here] = low.astype(F32)
     for part, sums in ((1, key_sum), (2, value_sum)):
         low = sums[...].T.astype(BF16)
         grads[row, part, head] = low
-        flat[place_of(part), :] = low.astype(F32)
+        spare[place_of(part), :] = low.astype(F32)
 
     to_self(row, head).start()
     for m in range(1, 4):
         to_peer(row, head, m).start()
 
+    own_features = 3 * own
+
     @pl.when((head == heads - 1) & (row == 0))
     def _():
-        total[...] = jnp.dot(flat[...].astype(BF16), normed[0], preferred_element_type=F32)
+        total[...] = jnp.dot(spare[:own_features].astype(BF16), normed[0], preferred_element_type=F32)
 
     @pl.when((head == heads - 1) & (row > 0))
     def _():
-        total[...] += jnp.dot(flat[...].astype(BF16), normed[0], preferred_element_type=F32)
+        total[...] += jnp.dot(spare[:own_features].astype(BF16), normed[0], preferred_element_type=F32)
+
+    def store_tokens(r):
+        return pltpu.make_async_copy(grad_here.at[r], grad_tokens.at[r], store_sem.at[r])
+
+    def input_grad(r):
+        for h in range(heads):
+            to_self(r, h).wait()
+            for m in range(1, 4):
+                to_peer(r, h, m).wait()
+        grad_normed = jnp.zeros((width, local), F32)
+        for part in range(3):
+            for place in range(4):
+                for h in range(heads):
+                    start = (place * heads + h) * size
+                    features[start : start + size] = token_got[r, part, place, h].astype(F32)
+            low = features[...].astype(BF16)
+            grad_normed += jnp.dot(weights[part], low, preferred_element_type=F32)
+            if part != 1:
+                lanes = slice(part * width, (part + 1) * width)
+                ones = jnp.ones((8, local), BF16)
+                feature_sums[:, lanes] += lax.dot_general(ones, low, (((1,), (1,)), ((), ())), preferred_element_type=F32)
+        grad_normed = grad_normed.T
+        normal, inverse = normalize(tokens_here[r].astype(F32))
+        seg_row = seg[r : r + 1, pl.ds(pl.multiple_of(seq * local, 128), local)]
+        scale_a = per_token(slot_col, seg_row, table[r, :, width : 2 * width])
+        grad_here[r] = middle_here[r] + normalize_back(normal, inverse, grad_normed * (1.0 + scale_a))
+        store_tokens(r).start()
+        late = [per_slot(slot_col, seg_row, piece) for piece in (grad_normed, grad_normed * normal)]
+        slots = jnp.concatenate(late + [slot_sums[r]], axis=1)
+        pick = lax.broadcasted_iota(jnp.int32, (images, slots.shape[0]), 0) == image_index[r : r + 1, :]
+        image_sums[...] += jnp.dot(pick.astype(F32), slots, precision=lax.Precision.HIGHEST, preferred_element_type=F32)
 
     @pl.when(last)
     def _():
-        turned[...] = total[...].T
+        spare[:, :own_features] = total[...].T
         for place in range(4):
             other = pl.multiple_of((2 * place + 1 - core) * depth, 8)
-            core_out[place] = turned[pl.ds(other, depth), :].astype(BF16)
+            core_out[place] = spare[pl.ds(other, depth), :own_features].astype(BF16)
         core_copy.start()
-        for copy in proj_copies:
-            copy.wait()
-        mine = proj[chip]
+        end(proj_copies)
+        mine = proj_own[...]
         for k in range(3):
             mine = mine + proj_got[k].astype(F32)
         for place in range(4):
             seq_out[place] = mine[:, place * own : (place + 1) * own].astype(BF16)
-        for copy in seq_copies:
-            copy.start()
+        go(seq_copies)
+        for place in range(4):
+
+            @pl.when(seq == place)
+            def _():
+                proj_ref[...] = mine[:, place * own : (place + 1) * own]
+
         down_copy.wait()
         left, right = down_out[core], down_got[...]
         left, right = jnp.where(core == 0, left, right), jnp.where(core == 0, right, left)
@@ -1257,36 +1396,147 @@
         core_copy.wait()
         for place in range(4):
             same = pl.multiple_of((2 * place + core) * depth, 8)
-            qkv_ref[place] = turned[pl.ds(same, depth), :] + core_got[place].astype(F32)
+            core_out[place] = (spare[pl.ds(same, depth), :own_features] + core_got[place].astype(F32)).astype(BF16)
+        same = pl.multiple_of(group * depth, 8)
+        qkv_own[...] = spare[pl.ds(same, depth), :own_features] + core_got[chip].astype(F32)
+        go(chip_copies)
+
+        end(load_weights + [load_tokens, load_middle])
+        for r in range(rows):
+            input_grad(r)
+        go(load_ada)
+
         for place in range(4):
-
-            @pl.when(seq == place)
-            def _():
-                proj_ref[...] = mine[:, place * own : (place + 1) * own]
-
+            mod[place] = image_sums[:, place * columns : (place + 1) * columns]
+        lines[...] = jnp.zeros_like(lines)
+        for line in range(8):
+            if line < 2:
+                value = feature_sums[0:1, 2 * line * width : (2 * line + 1) * width]
+            else:
+                value = (proj_bias[...], *(up_bias[k] for k in range(4)), down_bias[...])[line - 2]
+            lines[line // 2, line % 2 : line % 2 + 1, :width] = value
+        go(mod_copies + line_copies)
         for m, copy in enumerate(seq_copies):
             copy.wait()
             proj_ref[...] += seq_got[m].astype(F32)
+        sums = mod[seq]
+        for m, copy in enumerate(mod_copies):
+            copy.wait()
+            sums = sums + got[m]
+        low = sums.astype(BF16)
+        low_all[chip, core] = low
+        go([low_core] + low_chips)
+        small = lines[seq]
+        for m, copy in enumerate(line_copies):
+            copy.wait()
+            small = small + lines_got[m]
+        small_core[core] = small
+        small_core[core, 2:3] = jnp.sum(sums, axis=0, keepdims=True)
+        small_over.start()
+        end(load_ada)
+        term = jnp.dot(low[:, :width], weights[0], preferred_element_type=F32)
+        term += jnp.dot(low[:, width:], weights[1, : columns - width], preferred_element_type=F32)
+        cond_all[seq] = term
+        go(cond_copies)
+        end(chip_copies + column_copies)
+        mine = qkv_own[...]
+        for k in range(3):
+            mine = mine + chip_got[k].astype(F32)
+        for part in range(3):
+            piece_out[part] = mine[:, part * own : (part + 1) * own]
+
+        def piece(part):
+            index = part * 4 + seq
+            target, place = lax.div(index, 3), lax.rem(index, 3)
+            copy = send_to(
+                piece_out.at[part], piece_got.at[place], other_sent.at[base + part], other_came.at[base + place], {"seq": target}
+            )
+            return copy, target, place
+
+        def arriving(place):
+            source = lax.rem(3 * seq + place, 4)
+            copy = send_to(
+                piece_out.at[0], piece_got.at[place], other_sent.at[base], other_came.at[base + place], {"seq": source}
+            )
+            return copy, source
+
+        for part in range(3):
+            copy, target, place = piece(part)
+
+            @pl.when(target != seq)
+            def _():
+                copy.start()
+
+            @pl.when(target == seq)
+            def _():
+                piece_got[place] = piece_out[part]
+
+        small_over.wait()
+        small_chip[chip] = small_core[0] + small_core[1]
+        go(small_chips)
+        for came_in, going_on in zip(low_chips, low_on):
+            came_in.wait()
+            going_on.start()
+        end(small_chips)
+        small_seq[seq] = (small_chip[0] + small_chip[1]) + (small_chip[2] + small_chip[3])
+        go(small_copies)
+        end([low_core] + low_on)
+        gathered = jnp.concatenate([low_all[m // 2, m % 2] for m in range(8)], axis=0)
+        blocks = jnp.concatenate([column_got[m] for m in range(8)], axis=0)
+        ada_ref[...] = lax.dot_general(blocks, gathered, (((0,), (0,)), ((), ())), preferred_element_type=F32)
+        for part in range(3):
+            copy, target, place = piece(part)
+
+            @pl.when(target != seq)
+            def _():
+                copy.wait_send()
+
+        for place in range(3):
+            copy, source = arriving(place)
+
+            @pl.when(source != seq)
+            def _():
+                copy.wait_recv()
+
+        for place in range(3):
+            qkv_ref[:, place * own : (place + 1) * own] = piece_got[place]
+        end(cond_copies)
+        value = conditioning[...].astype(F32)
+        gate = 1.0 / (1.0 + jnp.exp(-value))
+        sums = (cond_all[0] + cond_all[1]) + (cond_all[2] + cond_all[3])
+        cond_ref[...] = sums * gate * (1.0 + value * (1.0 - gate))
+        end(small_copies)
+        for place in range(4):
+            ada_bias_ref[pl.ds(place * columns, columns)] = small_seq[place, 2]
+        qv_bias_ref[...] = small_seq[0, 0:2, :width]
+        proj_bias_ref[...] = small_seq[1, 0, :width]
+        for line in range(3, 7):
+            up_bias_ref[pl.ds((line - 3) * width, width)] = small_seq[line // 2, line % 2, :width]
+        down_bias_ref[...] = small_seq[3, 1, :width]
         for r in range(rows):
-            for h in range(heads):
-                to_self(r, h).wait()
-                for m in range(1, 4):
-                    to_peer(r, h, m).wait()
-
-
-def attend_back_reduce(packed, out, grad_out, lse, col, row, normed, proj, down, block, inner):
+            store_tokens(r).wait()
+
+
+def attend_back_and_finish(packed, out, grad_out, lse, col, row, normed, *rest):
+    proj_own, proj_low, down, seg, table, slot_sums, image_index, conditioning, biases, tokens, grad_middle, weight, ada = rest
     rows, _, heads, size, length = packed.shape
     width = normed.shape[2]
-    depth, own, features = width // 8, width // 4, 3 * heads * size
+    depth, own, features, local = width // 8, width // 4, 3 * heads * size, length // 4
     half = down.shape[1] // 2
+    images, columns = conditioning.shape[0], ada.shape[0]
     part = lambda j: pl.BlockSpec((1, None, 1, size, length), lambda r, h: (r, j, h, 0, 0))
     whole = pl.BlockSpec((1, 1, size, length), lambda r, h: (r, h, 0, 0))
-    fixed = lambda *dims: pl.BlockSpec(dims, lambda r, h: (0,) * len(dims))
+    single = pl.Buffered(buffer_count=1)
+    fixed = lambda *dims: pl.BlockSpec(dims, lambda r, h: (0,) * len(dims), pipeline_mode=single)
+    result = lambda *dims: pl.BlockSpec(dims, lambda r, h: (0,) * len(dims))
+    far = pl.BlockSpec(memory_space=pl.ANY)
     shape = jax.ShapeDtypeStruct
+    vmem = lambda dtype, *dims: pltpu.VMEM(dims, dtype)
     count = rows * heads
+    copies = 3 + 3 + 1 + 1 + 3 + 7 + 3 + 3 + 1 + 3 + 3 + 1 + 3 + 3 + 3 + 3
     dma = lambda n: pltpu.SemaphoreType.DMA((n,))
     return pl.pallas_call(
-        partial(attend_back_reduce_kernel, block, inner, size**-0.5),
+        partial(back_kernel, 256, 512, size**-0.5),
         grid=(rows, heads),
         in_specs=[
             pl.BlockSpec((1, length, 1), lambda r, h: (r, 0, 0)),
@@ -1297,323 +1547,72 @@
             whole,
             whole,
             pl.BlockSpec((1, 1, 1, length), lambda r, h: (r, h, 0, 0)),
-            pl.BlockSpec((1, length, width), lambda r, h: (r, 0, 0)),
+            pl.BlockSpec((1, length, width), lambda r, h: (r, 0, 0), pipeline_mode=single),
+            fixed(depth, width),
             fixed(4, depth, width),
             fixed(depth, 2 * half),
+            fixed(*seg.shape),
+            fixed(*table.shape),
+            fixed(*slot_sums.shape),
+            fixed(*image_index.shape),
+            fixed(images, width),
+            fixed(1, width),
+            fixed(4, 1, width),
+            fixed(1, width),
+            far,
+            far,
+            far,
+            far,
         ],
-        out_specs=[pl.BlockSpec(memory_space=pl.ANY), fixed(4, depth, features), fixed(depth, own), fixed(own, half)],
+        out_specs=[
+            far,
+            result(depth, own),
+            result(own, half),
+            result(depth, columns),
+            result(images, width),
+            result(4 * columns),
+            result(2, width),
+            result(width),
+            result(4 * width),
+            result(width),
+            result(depth, features),
+        ],
         out_shape=[
-            shape((rows, 3, 4, heads, size, length // 4), BF16),
-            shape((4, depth, features), F32),
+            shape((rows, local, width), F32),
             shape((depth, own), F32),
             shape((own, half), F32),
+            shape((depth, columns), F32),
+            shape((images, width), F32),
+            shape((4 * columns,), F32),
+            shape((2, width), F32),
+            shape((width,), F32),
+            shape((4 * width,), F32),
+            shape((width,), F32),
+            shape((depth, features), F32),
         ],
         scratch_shapes=[
-            pltpu.VMEM((rows, 3, heads, size, length), BF16),
-            pltpu.VMEM((length, size), F32),
-            pltpu.VMEM((length, size), F32),
-            pltpu.VMEM((length, size), BF16),
-            pltpu.VMEM((length, size), BF16),
-            pltpu.VMEM((features, length), F32),
-            pltpu.VMEM((features, width), F32),
-            pltpu.VMEM((width, features), F32),
-            pltpu.VMEM((4, depth, features), BF16),
-            pltpu.VMEM((4, depth, features), BF16),
-            pltpu.VMEM((4, depth, width), BF16),
-            pltpu.VMEM((3, depth, width), BF16),
-            pltpu.VMEM((4, depth, own), BF16),
-            pltpu.VMEM((3, depth, own), BF16),
-            pltpu.VMEM((2, depth, half), F32),
-            pltpu.VMEM((depth, half), F32),
-            dma(3 * count),
-            dma(3 * count),
-            dma(count),
-            dma(3),
-            dma(3),
-            dma(3),
-            dma(3),
-            dma(2),
-            dma(2),
-        ],
-        compiler_params=pltpu.CompilerParams(vmem_limit_bytes=VMEM_LIMIT, collective_id=3, has_side_effects=True),
-        cost_estimate=pl.CostEstimate(
-            flops=20 * rows * heads * length * length * 128,
-            bytes_accessed=16 * rows * heads * length * size,
-            transcendentals=rows * heads * length * length,
-        ),
-    )(col, row, packed, packed, packed, out, grad_out, lse, normed, proj, down)
-
-
-def last_kernel(
-    slot_col,
-    seg,
-    table,
-    grads,
-    weight,
-    tokens,
-    grad_middle,
-    slot_sums,
-    pick,
-    conditioning,
-    biases,
-    qkv,
-    cond,
-    ada,
-    grad_tokens,
-    ada_ref,
-    cond_ref,
-    ada_bias_ref,
-    qv_bias_ref,
-    proj_bias_ref,
-    up_bias_ref,
-    down_bias_ref,
-    qkv_ref,
-    ada_here,
-    image_sums,
-    feature_sums,
-    mod,
-    got,
-    lines,
-    lines_got,
-    low_all,
-    small_core,
-    small_chip,
-    small_seq,
-    cond_all,
-    column_got,
-    chip_out,
-    chip_got,
-    piece_out,
-    piece_got,
-    ada_came,
-    sent,
-    came,
-):
-    step, rows = pl.program_id(0), pl.num_programs(0)
-    seq, group = lax.axis_index("seq"), lax.axis_index("rows")
-    width = tokens.shape[-1]
-    images = image_sums.shape[0]
-    columns = mod.shape[2]
-    own = width // 4
-    chip, core = lax.div(group, 2), lax.rem(group, 2)
-    seq_peers = peers_of(seq)
-    to_seq = [{"seq": peer} for peer in seq_peers]
-    rows_peers = [lax.rem(group + m, 8) for m in range(8)]
-    to_row = [{"rows": peer} for peer in rows_peers]
-    chips = [lax.rem(chip + k, 4) for k in range(4)]
-    load_ada = pltpu.make_async_copy(ada, ada_here, ada_came)
-    used = [0]
-
-    def copy_to(source, target, device):
-        used[0] += 1
-        return send_to(source, target, sent.at[used[0] - 1], came.at[used[0] - 1], device)
-
-    chip_copies = [copy_to(chip_out.at[chips[k]], chip_got.at[k - 1], {"rows": 2 * chips[k] + core}) for k in range(1, 4)]
-    column_copies = [copy_to(cond.at[rows_peers[m]], column_got.at[group], to_row[m]) for m in range(1, 8)]
-    mod_copies = [copy_to(mod.at[seq_peers[m]], got.at[m], to_seq[m]) for m in range(3)]
-    line_copies = [copy_to(lines.at[seq_peers[m]], lines_got.at[m], to_seq[m]) for m in range(3)]
-    core_peer = {"rows": group + 1 - 2 * core}
-    chip_peers = [{"rows": 2 * chips[k] + core} for k in range(4)]
-    low_core = copy_to(low_all.at[chip, core], low_all.at[chip, core], core_peer)
-    low_chips = [copy_to(low_all.at[chip, core], low_all.at[chip, core], chip_peers[k]) for k in range(1, 4)]
-    before = [lax.rem(chip + 4 - k, 4) for k in range(4)]
-    low_on = [copy_to(low_all.at[before[k], core], low_all.at[before[k], core], core_peer) for k in range(1, 4)]
-    small_over = copy_to(small_core.at[core], small_core.at[core], core_peer)
-    small_chips = [copy_to(small_chip.at[chip], small_chip.at[chip], chip_peers[k]) for k in range(1, 4)]
-    small_copies = [copy_to(small_seq.at[seq], small_seq.at[seq], to_seq[m]) for m in range(3)]
-    cond_copies = [copy_to(cond_all.at[seq], cond_all.at[seq], to_seq[m]) for m in range(3)]
-    base = used[0]
-
-    @pl.when(step == 0)
-    def _():
-        load_ada.start()
-        greet(to_seq + to_row[1:])
-        chip_out[...] = qkv[...].astype(BF16)
-        for copy in chip_copies + column_copies:
-            copy.start()
-        column_got[group] = cond[group]
-        image_sums[...] = jnp.zeros_like(image_sums)
-        feature_sums[...] = jnp.zeros_like(feature_sums)
-
-    grad_low = grads[0]
-    grad_normed = jnp.dot(weight[...], grad_low, preferred_element_type=F32).T
-    ones = jnp.ones((8, grad_low.shape[1]), BF16)
-    feature_sums[...] += lax.dot_general(ones, grad_low, (((1,), (1,)), ((), ())), preferred_element_type=F32)
-    normal, inverse = normalize(tokens[0].astype(F32))
-    scale_a = per_token(slot_col[...], seg[0], table[0, :, width : 2 * width])
-    grad_tokens[0] = grad_middle[0] + normalize_back(normal, inverse, grad_normed * (1.0 + scale_a))
-    late = [per_slot(slot_col[...], seg[0], piece) for piece in (grad_normed, grad_normed * normal)]
-    slots = jnp.concatenate(late + [slot_sums[0]], axis=1)
-    image_sums[...] += jnp.dot(pick[0], slots, precision=lax.Precision.HIGHEST, preferred_element_type=F32)
-
-    @pl.when(step == rows - 1)
-    def _():
-        for place in range(4):
-            mod[place] = image_sums[:, place * columns : (place + 1) * columns]
-        lines[...] = jnp.zeros_like(lines)
-        for line in range(8):
-            value = biases[line : line + 1]
-            if line < 2:
-                value = feature_sums[0:1, 2 * line * width : (2 * line + 1) * width]
-            lines[line // 2, line % 2 : line % 2 + 1, :width] = value
-        for copy in mod_copies + line_copies:
-            copy.start()
-        total = mod[seq]
-        for m, copy in enumerate(mod_copies):
-            copy.wait()
-            total = total + got[m]
-        low = total.astype(BF16)
-        low_all[chip, core] = low
-        low_core.start()
-        for copy in low_chips:
-            copy.start()
-        small = lines[seq]
-        for m, copy in enumerate(line_copies):
-            copy.wait()
-            small = small + lines_got[m]
-        small_core[core] = small
-        small_core[core, 2:3] = jnp.sum(total, axis=0, keepdims=True)
-        small_over.start()
-        load_ada.wait()
-        cond_all[seq] = jnp.dot(low, ada_here[...], preferred_element_type=F32)
-        for copy in cond_copies:
-            copy.start()
-        for copy in chip_copies:
-            copy.wait()
-        for copy in column_copies:
-            copy.wait()
-        mine = qkv[chip]
-        for k in range(3):
-            mine = mine + chip_got[k].astype(F32)
-        for part in range(3):
-            piece_out[part] = mine[:, part * own : (part + 1) * own]
-
-        def piece(part):
-            index = part * 4 + seq
-            target, place = lax.div(index, 3), lax.rem(index, 3)
-            copy = send_to(piece_out.at[part], piece_got.at[place], sent.at[base + part], came.at[base + place], {"seq": target})
-            return copy, target, place
-
-        def arriving(place):
-            source = lax.rem(3 * seq + place, 4)
-            copy = send_to(piece_out.at[0], piece_got.at[place], sent.at[base], came.at[base + place], {"seq": source})
-            return copy, source
-
-        for part in range(3):
-            copy, target, place = piece(part)
-
-            @pl.when(target != seq)
-            def _():
-                copy.start()
-
-            @pl.when(target == seq)
-            def _():
-                piece_got[place] = piece_out[part]
-
-        small_over.wait()
-        small_chip[chip] = small_core[0] + small_core[1]
-        for copy in small_chips:
-            copy.start()
-        for came_in, going_on in zip(low_chips, low_on):
-            came_in.wait()
-            going_on.start()
-        for copy in small_chips:
-            copy.wait()
-        small_seq[seq] = (small_chip[0] + small_chip[1]) + (small_chip[2] + small_chip[3])
-        for copy in small_copies:
-            copy.start()
-        low_core.wait()
-        for copy in low_on:
-            copy.wait()
-        gathered = jnp.concatenate([low_all[m // 2, m % 2] for m in range(8)], axis=0)
-        blocks = jnp.concatenate([column_got[m] for m in range(8)], axis=0)
-        ada_ref[...] = lax.dot_general(blocks, gathered, (((0,), (0,)), ((), ())), preferred_element_type=F32)
-        for part in range(3):
-            copy, target, place = piece(part)
-
-            @pl.when(target != seq)
-            def _():
-                copy.wait_send()
-
-        for place in range(3):
-            copy, source = arriving(place)
-
-            @pl.when(source != seq)
-            def _():
-                copy.wait_recv()
-
-        for place in range(3):
-            qkv_ref[:, place * own : (place + 1) * own] = piece_got[place]
-        for copy in cond_copies:
-            copy.wait()
-        term = (cond_all[0] + cond_all[1]) + (cond_all[2] + cond_all[3])
-        value = conditioning[...]
-        gate = 1.0 / (1.0 + jnp.exp(-value))
-        cond_ref[...] = term * gate * (1.0 + value * (1.0 - gate))
-        for copy in small_copies:
-            copy.wait()
-        for place in range(4):
-            ada_bias_ref[:, place * columns : (place + 1) * columns] = small_seq[place, 2:3]
-        qv_bias_ref[...] = small_seq[0, 0:2, :width]
-        proj_bias_ref[...] = small_seq[1, 0:1, :width]
-        for line in range(3, 7):
-            up_bias_ref[:, (line - 3) * width : (line - 2) * width] = small_seq[line // 2, line % 2 : line % 2 + 1, :width]
-        down_bias_ref[...] = small_seq[3, 1:2, :width]
-
-
-def finish_all(slot_col, seg, table, grads, weight, tokens, grad_middle, slot_sums, pick, conditioning, biases, qkv, cond, ada):
-    rows, length, width = tokens.shape
-    images, columns = conditioning.shape[0], ada.shape[0]
-    depth, own = width // 8, width // 4
-    fixed = lambda *dims: pl.BlockSpec(dims, lambda r: (0,) * len(dims), pipeline_mode=pl.Buffered(buffer_count=1))
-    result = lambda *dims: pl.BlockSpec(dims, lambda r: (0,) * len(dims))
-    row = lambda *dims: pl.BlockSpec((1,) + dims, lambda r: (r, 0, 0))
-    shape = jax.ShapeDtypeStruct
-    vmem = lambda dtype, *dims: pltpu.VMEM(dims, dtype)
-    copies = 3 + 7 + 3 + 3 + 1 + 3 + 3 + 1 + 3 + 3 + 3 + 3
-    return pl.pallas_call(
-        last_kernel,
-        grid=(rows,),
-        in_specs=[
-            fixed(*slot_col.shape),
-            row(1, length),
-            row(*table.shape[1:]),
-            row(3 * width, length),
-            fixed(width, 3 * width),
-            row(length, width),
-            row(length, width),
-            row(*slot_sums.shape[1:]),
-            row(*pick.shape[1:]),
-            fixed(images, width),
-            fixed(8, width),
-            fixed(4, depth, 3 * own),
-            fixed(8, images, depth),
-            pl.BlockSpec(memory_space=pl.ANY),
-        ],
-        out_specs=[
-            row(length, width),
-            result(depth, columns),
-            result(images, width),
-            result(1, 4 * columns),
-            result(2, width),
-            result(1, width),
-            result(1, 4 * width),
-            result(1, width),
-            result(depth, 3 * own),
-        ],
-        out_shape=[
-            shape((rows, length, width), F32),
-            shape((depth, columns), F32),
-            shape((images, width), F32),
-            shape((1, 4 * columns), F32),
-            shape((2, width), F32),
-            shape((1, width), F32),
-            shape((1, 4 * width), F32),
-            shape((1, width), F32),
-            shape((depth, 3 * own), F32),
-        ],
-        scratch_shapes=[
-            vmem(BF16, columns, width),
+            vmem(BF16, rows, 3, heads, size, length),
+            vmem(BF16, rows, 3, 4, heads, size, local),
+            vmem(F32, length, size),
+            vmem(F32, length, size),
+            vmem(BF16, length, size),
+            vmem(BF16, length, size),
+            vmem(F32, features, width),
+            vmem(F32, width, length),
+            vmem(BF16, 4, depth, features),
+            vmem(BF16, 4, depth, features),
+            vmem(BF16, 3, depth, width),
+            vmem(BF16, 4, depth, own),
+            vmem(BF16, 3, depth, own),
+            vmem(F32, 2, depth, half),
+            vmem(F32, depth, half),
+            vmem(F32, depth, features),
+            vmem(BF16, 3, depth, features),
+            vmem(BF16, 3, width, width),
+            vmem(BF16, rows, local, width),
+            vmem(F32, rows, local, width),
+            vmem(F32, rows, local, width),
+            vmem(F32, width, local),
             vmem(F32, images, 6 * width),
             vmem(F32, 8, 3 * width),
             vmem(F32, 4, images, columns),
@@ -1626,23 +1625,52 @@
             vmem(F32, 4, 8, columns),
             vmem(F32, 4, images, width),
             vmem(BF16, 8, images, depth),
-            vmem(BF16, 4, depth, 3 * own),
-            vmem(BF16, 3, depth, 3 * own),
+            vmem(BF16, 8, images, depth),
             vmem(F32, 3, depth, own),
             vmem(F32, 3, depth, own),
-            pltpu.SemaphoreType.DMA,
-            pltpu.SemaphoreType.DMA((copies,)),
-            pltpu.SemaphoreType.DMA((copies,)),
+            dma(3 * count),
+            dma(3 * count),
+            dma(count),
+            dma(7),
+            dma(rows),
+            dma(copies),
+            dma(copies),
         ],
-        compiler_params=pltpu.CompilerParams(vmem_limit_bytes=VMEM_LIMIT, collective_id=5, has_side_effects=True),
-        cost_estimate=pl.CostEstimate(flops=5 * 10**9, bytes_accessed=3 * 10**7, transcendentals=0),
-    )(slot_col, seg, table, grads, weight, tokens, grad_middle, slot_sums, pick, conditioning, biases, qkv, cond, ada)
+        compiler_params=pltpu.CompilerParams(vmem_limit_bytes=VMEM_LIMIT, collective_id=3, has_side_effects=True),
+        cost_estimate=pl.CostEstimate(
+            flops=20 * rows * heads * length * length * 128,
+            bytes_accessed=16 * rows * heads * length * size,
+            transcendentals=rows * heads * length * length,
+        ),
+    )(
+        col,
+        row,
+        packed,
+        packed,
+        packed,
+        out,
+        grad_out,
+        lse,
+        normed,
+        proj_own,
+        proj_low,
+        down,
+        seg,
+        table,
+        slot_sums,
+        image_index,
+        conditioning,
+        *biases,
+        tokens,
+        grad_middle,
+        weight,
+        ada,
+    )
 
 
 def forward_kernel(
     block,
-    slot_col,
-    image_col,
+    image_index,
     seg,
     fill,
     conditioning,
@@ -1711,7 +1739,8 @@
     _, parts, heads, size, length = packed_all.shape
     own, depth, half = heads * size, width // 8, local // 2
     columns = ada_here.shape[0]
-    images, slots = conditioning.shape[0], image_col.shape[1]
+    images, slots = conditioning.shape[0], image_index.shape[1]
+    slot_col = slot_column(slots)
     scale = size**-0.5 * LOG2E
     seq = lax.axis_index("seq")
     core = lax.rem(lax.axis_index("rows"), 2)
@@ -1762,12 +1791,12 @@
     for m in range(4):
         lanes = pl.ds(pl.multiple_of(places[m] * local, 128), local)
         found = seg[:, lanes]
-        where = places[m] * local + lax.broadcasted_iota(jnp.int32, (rows, local), 1)
-        code = jnp.where(where < fill[...], found, -1 - where)
+        where = places[m] * local + lax.broadcasted_iota(jnp.int32, (1, local), 1)
         for r in range(rows):
+            code = jnp.where(where < fill[r], found[r : r + 1], -1 - where)
             seg_all[r, m] = found[r : r + 1]
-            code_row[r, :, m * local : (m + 1) * local] = code[r : r + 1]
-            column = jnp.broadcast_to(code[r : r + 1].astype(F32), (128, local)).T[:, :1]
+            code_row[r, :, m * local : (m + 1) * local] = code
+            column = jnp.broadcast_to(code.astype(F32), (128, local)).T[:, :1]
             code_col[r, m * local : (m + 1) * local] = column.astype(jnp.int32)
 
     for part in range(3):
@@ -1783,14 +1812,16 @@
     go([forward(0, m) for m in (1, 2)] + [direct(1, m) for m in (1, 2)])
 
     end(mod_copies)
+    bias_all = ada_bias[...].astype(F32).reshape(1, 4 * columns)
+    proj_line = proj_bias[...].astype(F32).reshape(1, width)
     for place in range(4):
         lanes = slice(place * columns, (place + 1) * columns)
-        table[:, lanes] = mod_all[place] + ada_bias[:, lanes].astype(F32)
+        table[:, lanes] = mod_all[place] + bias_all[:, lanes]
     stacked = jnp.concatenate(split_low(table[...]), axis=0)
-    image_row = lax.rem(lax.broadcasted_iota(jnp.int32, (slots, 3 * images), 1), images)
+    image_col = lax.rem(lax.broadcasted_iota(jnp.int32, (3 * images, slots), 0), images)
     for r in range(rows):
-        picked = (image_col[r] == image_row).astype(BF16)
-        table_ref[r] = jnp.dot(picked, stacked, preferred_element_type=F32)
+        picked = (image_col == image_index[r : r + 1]).astype(BF16)
+        table_ref[r] = lax.dot_general(picked, stacked, (((0,), (0,)), ((), ())), preferred_element_type=F32)
 
     def stores(r, m):
         index = r * 4 + m
@@ -1801,7 +1832,7 @@
         )
 
     def work(r, m):
-        mods = per_token(slot_col[...], seg_all[r, m], table_ref[r, :, : 2 * width])
+        mods = per_token(slot_col, seg_all[r, m], table_ref[r, :, : 2 * width])
         normal, _ = normalize(here[r, m].astype(F32))
         normed = (normal * (1.0 + mods[:, width:]) + mods[:, :width]).astype(BF16)
         normed_all[r, m] = normed
@@ -1886,9 +1917,9 @@
                 flat[start : start + size] = attended_got[r, place, h].astype(F32)
         features = flat[...].astype(BF16)
         features_all[r] = features
-        mods = per_token(slot_col[...], seg_all[r, 0], table_ref[r, :, 2 * width :])
+        mods = per_token(slot_col, seg_all[r, 0], table_ref[r, :, 2 * width :])
         gate_a, shift_b, scale_b, gate_b = (mods[:, k * width : (k + 1) * width] for k in range(4))
-        branch = lax.dot_general(features, proj_here[...], (((0,), (0,)), ((), ())), preferred_element_type=F32) + proj_bias[...]
+        branch = lax.dot_general(features, proj_here[...], (((0,), (0,)), ((), ())), preferred_element_type=F32) + proj_line
         middle = here[r, 0].astype(F32) + gate_a * branch
         branch_all[r] = branch
         middle_all[r] = middle
@@ -1915,10 +1946,10 @@
         end(last_stores(r))
 
 
-def before_feed_forward(slot_col, image_col, seg, fill, conditioning, ada_bias, qv_bias, proj_bias, tokens, ada, weight, proj, cotangent):
+def before_feed_forward(image_index, seg, fill, conditioning, ada_bias, qv_bias, proj_bias, tokens, ada, weight, proj, cotangent):
     rows, local, width = tokens.shape
     length = 4 * local
-    images, slots = conditioning.shape[0], image_col.shape[1]
+    images, slots = conditioning.shape[0], image_index.shape[1]
     heads, size = HEADS // 4, width // HEADS
     columns = ada.shape[0]
     shape = jax.ShapeDtypeStruct
@@ -1927,7 +1958,7 @@
     dma = lambda *dims: pltpu.SemaphoreType.DMA(dims)
     return pl.pallas_call(
         partial(forward_kernel, 512),
-        in_specs=[near] * 8 + [far] * 5,
+        in_specs=[near] * 2 + [pl.BlockSpec(memory_space=pltpu.SMEM)] + [near] * 4 + [far] * 5,
         out_specs=[far] * 10 + [near] * 5,
         out_shape=[
             shape((rows, 4, local, width), BF16),
@@ -1987,7 +2018,7 @@
         ],
         compiler_params=pltpu.CompilerParams(vmem_limit_bytes=VMEM_LIMIT, collective_id=6, has_side_effects=True),
         cost_estimate=pl.CostEstimate(flops=2 * 10**10, bytes_accessed=4 * 10**7, transcendentals=0),
-    )(slot_col, image_col, seg, fill, conditioning, ada_bias, qv_bias, proj_bias, tokens, ada, weight, proj, cotangent)
+    )(image_index, seg, fill, conditioning, ada_bias, qv_bias, proj_bias, tokens, ada, weight, proj, cotangent)
 
 
 def gather_seq(values):
@@ -2087,8 +2118,6 @@
     hidden_size = up_weight.shape[1]
     depth = width // groups
 
-    slot_ids = lax.iota(jnp.int32, image_index.shape[1])
-    slot_col = jnp.tile(slot_ids, 3)[:, None]
     (
         normed_all,
         packed,
@@ -2106,14 +2135,13 @@
         log_totals,
         part_down_bias,
     ) = before_feed_forward(
-        slot_col,
-        image_index[:, :, None],
+        image_index,
         segment_ids,
-        row_fill[:, None],
+        row_fill,
         conditioning,
-        ada_bias[None],
+        ada_bias,
         qv_bias,
-        proj_bias.astype(F32)[None],
+        proj_bias,
         tokens,
         ada_weight.T,
         qkv_weight,
@@ -2121,19 +2149,15 @@
         cotangent,
     )
     normed_all = normed_all.reshape(row_count, full_len, width)
-    cond_wide = conditioning.astype(F32)
-    cond_cols = jax.nn.silu(cond_wide).astype(BF16).reshape(image_count, groups, depth).transpose(1, 0, 2)
-    seg_row = lax.dynamic_slice_in_dim(segment_ids, seq_index * local_len, local_len, 1)[:, None, :]
     out_sum, grad_sum, part_up_bias, grad_up_weight, down_turned = feed_forward_reduce(
-        normed_b, grad_out, normed_turned, grad_turned, up_weight, down_weight, up_bias.astype(F32)
+        normed_b, grad_out, normed_turned, grad_turned, up_weight, down_weight, up_bias
     )
-    block_out, grad_middle, slot_sums, part_proj_bias, grad_view, proj_both = after_feed_forward(
-        slot_col,
-        seg_row,
+    block_out, grad_middle, slot_sums, part_proj_bias, grad_view, proj_own, proj_low = after_feed_forward(
+        segment_ids,
         slot_mod,
         attended_tok,
         proj_weight,
-        down_bias.astype(F32)[None],
+        down_bias,
         out_sum,
         grad_sum,
         middle,
@@ -2141,16 +2165,10 @@
         cotangent,
     )
     grad_view = grad_view.reshape(row_count, heads_dev, head_size, full_len)
-    grad_sent, qkv_both, grad_proj_weight, grad_down_weight = attend_back_reduce(
-        packed, attended, grad_view, log_totals, code_col, code_row, normed_all, proj_both, down_turned, 256, 512
-    )
-    grad_flat = grad_sent.reshape(row_count, 3 * width, local_len)
-    pick = (image_index[:, None, :] == lax.iota(jnp.int32, image_count)[None, :, None]).astype(F32)
-    biases = jnp.concatenate(
-        [jnp.zeros((2, width), F32), part_proj_bias, part_up_bias.reshape(4, width), part_down_bias], axis=0
-    )
     (
         grad_tokens,
+        grad_proj_weight,
+        grad_down_weight,
         grad_ada_weight,
         grad_cond,
         grad_ada_bias,
@@ -2159,20 +2177,26 @@
         grad_up_bias,
         grad_down_bias,
         grad_qkv_weight,
-    ) = finish_all(
-        slot_col,
-        seg_row,
+    ) = attend_back_and_finish(
+        packed,
+        attended,
+        grad_view,
+        log_totals,
+        code_col,
+        code_row,
+        normed_all,
+        proj_own,
+        proj_low,
+        down_turned,
+        segment_ids,
         slot_mod,
-        grad_flat,
-        qkv_weight,
+        slot_sums,
+        image_index,
+        conditioning,
+        (part_proj_bias, part_up_bias, part_down_bias),
         tokens,
         grad_middle,
-        slot_sums,
-        pick,
-        cond_wide,
-        biases,
-        qkv_both,
-        cond_cols,
+        qkv_weight,
         ada_weight.T,
     )
     return (
@@ -2180,15 +2204,15 @@
         grad_tokens,
         grad_cond,
         grad_ada_weight,
-        grad_ada_bias[0],
+        grad_ada_bias,
         grad_qkv_weight,
         grad_qv_bias,
         grad_proj_weight,
-        grad_proj_bias[0],
+        grad_proj_bias,
         grad_up_weight,
-        grad_up_bias[0],
+        grad_up_bias,
         grad_down_weight.T,
-        grad_down_bias[0],
+        grad_down_bias,
     )
 
 

time: 351 us -> 316 us (0.900)
  Pallas kernels: 318 us -> 298 us
  other arithmetic: 8.21 us -> 0 us
  local copies, waits for them, and re-layouts: 17.1 us -> 11.3 us
    pallas_call x4 -> x3, Pallas kernels: 205 us -> 185 us  [the longest x1 85.8 us: attend_back_and_finish(): pl.pallas_call(partial(back_kernel, 256, 512, size ** (-0.5)), grid=(rows...]
    broadcast_in_dim x7 -> x0, local copies, waits for them, and re-layouts: 6.45 us -> none  [the longest x1 1.36 us: on_square(): image_index[:, :, None]]
    pallas_call x4 -> x0, other arithmetic: 5.55 us -> none  [finish_all(): pl.pallas_call(last_kernel, grid=(rows,), in_specs=[fixed(*slot_col.shape...]
    unnamed x40 -> x39, local copies, waits for them, and re-layouts: 7.85 us -> 11.3 us
where the time goes in v1:
time: 316 us; the launch traced here: 311 us
  Pallas kernels  298 us (94%)
  local copies, waits for them, and re-layouts  11.3 us (4%)
    pallas_call x1, Pallas kernels, feed_forward_reduce(): pl.pallas_call(partial(mlp_reduce_kernel, tiles), grid=(tiles + STAGES,),...  113 us
    pallas_call x1, Pallas kernels, attend_back_and_finish(): pl.pallas_call(partial(back_kernel, 256, 512, size ** (-0.5)), grid=(rows...  85.8 us
    pallas_call x1, Pallas kernels, before_feed_forward(): pl.pallas_call(partial(forward_kernel, 512), in_specs=[near] * 2 + [pl.Bl...  75.2 us
    pallas_call x1, Pallas kernels, after_feed_forward(): pl.pallas_call(after_kernel, grid=(rows,), in_specs=[fixed(*seg.shape), r...  24.4 us
    unnamed x39, local copies, waits for them, and re-layouts  11.3 us

profile of v1, /device:TPU:0, one launch (start us, length us, event | category | flops | bytes accessed | tf_op | source)
XLA Modules:
  0.0 310.7 jit_solution(2143331677001208213)
XLA Ops:
  0.6 75.2 %shard_map.255 = (bf16[2,4,256,1152]{3,2,1,0:T(8,128)(2,1)}, bf16[2,3,4,72,1024]{4,3,2,1,0:T(8,128)(2,1)}, bf16[2,4,72,1024]{3,2,1,0:T(8,128)(2,1)}, bf16[2,1152...) custom-call(s32[2,8]{1,0:T(2,128)} %image_index.3, ...), custom_call_target="tpu_custom_call" | custom-call | flops 20000000000 | bytes 40000000 | tf_op jit(solution)/shard_map/pallas_call | solution.py:1959
  75.8 113.1 %shard_map.256 = (f32[512,1152]{1,0:T(8,128)}, f32[512,1152]{1,0:T(8,128)}, f32[4,1,1152]{2,1,0:T(1,128)}, f32[144,1152]{1,0:T(8,128)}, f32[144,1152]{1,0:T(8,128)}) custom-call(bf16[512,1152]{1,0:T(8,128)(2,1)} %get-tuple-element.53.normed, bf16[512,1152]{1,0:T(8,128)(2,1)} %get-tuple-element.54.grad_out, ...), custom_call_target="tpu_custom_call" | custom-call | flops 32614907904 | bytes 31850496 | tf_op jit(solution)/shard_map/pallas_call | solution.py:667
  189.0 24.4 %shard_map.257 = (bf16[2,256,1152]{2,1,0:T(8,128)(2,1)}, f32[2,256,1152]{2,1,0:T(8,128)}, f32[2,8,4608]{2,1,0:T(8,128)}, f32[1,1152]{1,0:T(1,128)}, bf16[2,288,1...) custom-call(s32[2,1024]{1,0:T(2,128)} %seg.5, f32[2,8,6912]{2,1,0:T(8,128)} %get-tuple-element.51.table, ...), custom_call_target="tpu_custom_call" | custom-call | flops 8000000000 | bytes 30000000 | tf_op jit(solution)/shard_map/pallas_call | solution.py:883
  213.4 0.0 copy-start.1
  213.4 85.8 %shard_map.258 = (f32[2,256,1152]{2,1,0:T(8,128)}, f32[144,288]{1,0:T(8,128)}, f32[288,576]{1,0:T(8,128)}, f32[144,1728]{1,0:T(8,128)}, f32[16,1152]{1,0:T(8,128...) custom-call(s32[2,1024,1]{2,1,0:T(8,128)} %get-tuple-element.62.code, ...), custom_call_target="tpu_custom_call" | custom-call | flops 21474836480 | bytes 9437184 | tf_op jit(solution)/shard_map/pallas_call | solution.py:1538
  299.1 0.0 copy-start
  299.1 0.0 copy-done.1
  299.1 1.0 copy.42
  300.2 1.1 copy-done
  301.2 0.0 copy-start.7
  301.2 0.0 copy-start.2
  301.2 0.0 copy-start.8
  301.2 0.0 copy-start.5
  301.2 1.4 copy.43
  302.6 0.0 copy-done.7
  302.6 0.0 copy-start.10
  302.6 0.0 copy-start.6
  302.6 0.0 copy-start.12
  302.6 0.0 copy-start.4
  302.7 0.6 copy.44
  303.3 0.0 copy-done.2
  303.3 0.0 copy-start.9
  303.3 0.0 copy-start.3
  303.3 1.0 copy.45
  304.3 0.0 copy-done.8
  304.3 0.0 copy-start.11
  304.3 0.6 copy.46
  304.9 0.0 copy-done.5
  304.9 0.8 copy.47
  305.7 0.0 copy-done.10
  305.7 0.6 copy.48
  306.3 0.0 copy-done.6
  306.3 0.7 copy.49
  307.0 0.0 copy-done.12
  307.0 0.6 copy.50
  307.6 0.0 copy-done.4
  307.6 0.8 copy.51
  308.4 0.0 copy-done.9
  308.4 0.6 copy.52
  309.0 0.0 copy-done.3
  309.0 0.9 copy.53
  309.9 0.0 copy-done.11
  309.9 0.6 copy.54
Async XLA Ops:
  213.4 85.8 %copy-start.1 = (bf16[2,256,1152]{2,1,0:T(8,128)(2,1)S(1)}, bf16[2,256,1152]{2,1,0:T(8,128)(2,1)}, u32[]{:S(2)}) copy-start(bf16[2,256,1152]{2,1,0:T(8,128)(2,1)} %get-tuple-element.102) | copy-start | bytes 3538948
  299.1 2.1 copy-start
  301.2 1.4 copy-start.7
  301.2 2.1 copy-start.2
  301.2 3.0 copy-start.8
  301.2 3.7 %copy-start.5 = (f32[144,864]{1,0:T(8,128)S(1)}, f32[144,864]{1,0:T(8,128)}, u32[]{:S(2)}) copy-start(f32[144,864]{1,0:T(8,128)} %get-tuple-element.107) | copy-start | bytes 1492996
  302.6 3.0 copy-start.10
  302.6 3.6 %copy-start.6 = (f32[144,288]{1,0:T(8,128)S(1)}, f32[144,288]{1,0:T(8,128)}, u32[]{:S(2)}) copy-start(f32[144,288]{1,0:T(8,128)} %get-tuple-element.109) | copy-start | bytes 497668
  302.6 4.3 %copy-start.12 = (f32[1152]{0:T(1024)S(1)}, f32[1152]{0:T(1024)}, u32[]{:S(2)}) copy-start(f32[1152]{0:T(1024)} %get-tuple-element.110) | copy-start | bytes 13828
  302.6 4.9 %copy-start.4 = (f32[144,1152]{1,0:T(8,128)S(1)}, f32[144,1152]{1,0:T(8,128)}, u32[]{:S(2)}) copy-start(f32[144,1152]{1,0:T(8,128)} %get-tuple-element.111) | copy-start | bytes 1990660
  303.3 5.1 %copy-start.9 = (f32[4608]{0:T(1024)S(1)}, f32[4608]{0:T(1024)}, u32[]{:S(2)}) copy-start(f32[4608]{0:T(1024)} %get-tuple-element.112) | copy-start | bytes 55300
  303.3 5.7 %copy-start.3 = (f32[288,576]{1,0:T(8,128)S(1)}, f32[288,576]{1,0:T(8,128)}, u32[]{:S(2)}) copy-start(f32[288,576]{1,0:T(8,128)} %get-tuple-element.87) | copy-start | bytes 1990660
  304.3 5.6 %copy-start.11 = (f32[1152]{0:T(1024)S(1)}, f32[1152]{0:T(1024)}, u32[]{:S(2)}) copy-start(f32[1152]{0:T(1024)} %get-tuple-element.114) | copy-start | bytes 13828
